TPU v7x, 128 devices: a whole 4x4x4 slice. The times are simulated.
128 devices in a mesh: grp: 4 (over z_hi, core), leaf: 32 (over z_lo, y, x).
Axes of the slice: x: 4, y: 4, z: 4 (z_hi: 2, z_lo: 2; z = z_hi * 2 + z_lo), core: 2. Of those that a mesh axis runs over, the one named last changes fastest.
Arguments:
- features: float32 [131072, 128], P(('grp', 'leaf')), may hold values from -6 to 6
- tree_order: int32 [128, 1024], P(('grp', 'leaf')), may hold values from 0 to 1023, each once within a row
- gain_leaf: float32 [128], replicated, may hold values from 0.1 to 1.9
- w_qkv_leaf: float32 [128, 384], replicated
- w_out_leaf: float32 [128, 128], replicated, may hold values from -0.5 to 0.5
- w_pool1: float32 [512, 256], replicated, may hold values from -0.5 to 0.5
- w_pool2: float32 [1024, 384], replicated, may hold values from -0.375 to 0.375
- w_pool3: float32 [1536, 512], replicated, may hold values from -0.21875 to 0.21875
- gain_coarse: float32 [512], replicated, may hold values from 0.1 to 1.9
- w_query: float32 [512, 512], replicated
- w_keyval: float32 [512, 1024], replicated
- w_out: float32 [512, 512], replicated, may hold values from -0.25 to 0.25
- cotangent: float32 [2048, 512], P(('grp', 'leaf')), may hold values from -6 to 6
Outputs:
- output: float32 [2048, 512], P(('grp', 'leaf'))
- grad_gain_leaf: float32 [128], replicated
- grad_qkv_leaf: float32 [128, 384], replicated
- grad_out_leaf: float32 [128, 128], replicated
- grad_pool1: float32 [512, 256], replicated
- grad_pool2: float32 [1024, 384], replicated
- grad_pool3: float32 [1536, 512], replicated
- grad_gain_coarse: float32 [512], replicated
- grad_query: float32 [512, 512], replicated
- grad_keyval: float32 [512, 1024], replicated
- grad_out: float32 [512, 512], replicated
Inputs may be any that keep to these rules, and one draw needn't show every extreme that they name: `tree_order`: each row lists the 1024 particles of one device, each once.
All inputs are finite; a program needn't handle non-finite values.
Results may differ from a plain program's by a relative error of at most 0.0003.
Values sent between devices are 32-bit elements; how exact they have to be, the bound alone decides.
No kernel may reach another device: no remote copies, remote signals or barrier semaphores. Data moves between devices by JAX's collectives and lax.ppermute only.
A program may use at most 128 MiB of HBM per device.

v0:
```python
import jax
import jax.numpy as jnp
from jax import lax
from jax.sharding import PartitionSpec as P

HEAD = 32
BALL = 128
ROOT_DEV = 2


MATMUL_ACCURACY = lax.Precision.HIGHEST


def matmul_high(left, right):
    return jnp.dot(left, right, precision=MATMUL_ACCURACY, preferred_element_type=jnp.float32)


def rms_scale(values, gain):
    return values * lax.rsqrt(jnp.mean(values * values, axis=-1, keepdims=True) + 1e-06) * gain


def leaf_front(ordered, gain_leaf, w_qkv_leaf, w_out_leaf, w_pool1, w_pool2, w_pool3):
    row_count, feature_width = ordered.shape
    head_count = feature_width // HEAD
    leaf_normed = rms_scale(ordered, gain_leaf)
    packed = matmul_high(leaf_normed, w_qkv_leaf).reshape(
        row_count // BALL, BALL, 3, head_count, HEAD
    )
    queries = packed[:, :, 0] * HEAD ** (-0.5)
    logit_scores = jnp.einsum(
        "bihd,bjhd->bhij", queries, packed[:, :, 1], precision=MATMUL_ACCURACY
    )
    attention_weights = jax.nn.softmax(logit_scores, axis=-1)
    attended = jnp.einsum(
        "bhij,bjhd->bihd", attention_weights, packed[:, :, 2], precision=MATMUL_ACCURACY
    )
    leaf_mixed = ordered + matmul_high(attended.reshape(row_count, feature_width), w_out_leaf)
    level_one = jax.nn.silu(matmul_high(leaf_mixed.reshape(row_count // 4, -1), w_pool1))
    level_two = jax.nn.silu(matmul_high(level_one.reshape(row_count // 16, -1), w_pool2))
    return matmul_high(level_two.reshape(row_count // 64, -1), w_pool3)


def attend_part(queries, keyval):
    query_total, feature_width = queries.shape
    key_count = keyval.shape[0]
    head_count = feature_width // HEAD
    scaled_scores = queries.reshape(query_total, head_count, HEAD) * HEAD ** (-0.5)
    key_slice = keyval[:, :feature_width].reshape(key_count, head_count, HEAD)
    value_slice = keyval[:, feature_width:].reshape(key_count, head_count, HEAD)
    logit_scores = jnp.einsum("kzo,czo->zkc", scaled_scores, key_slice, precision=MATMUL_ACCURACY)
    attention_weights = jax.nn.softmax(logit_scores, axis=-1)
    return jnp.einsum(
        "lut,tlk->ulk", attention_weights, value_slice, precision=MATMUL_ACCURACY
    ).reshape(query_total, feature_width)


def attend(queries, group_keyval, root_keyval):
    return attend_part(queries, group_keyval) + attend_part(queries, root_keyval)


def shards(
    features,
    tree_order,
    gain_leaf,
    w_qkv_leaf,
    w_out_leaf,
    w_pool1,
    w_pool2,
    w_pool3,
    gain_coarse,
    w_query,
    w_keyval,
    w_out,
    cotangent,
):
    ordered = features[tree_order[0]]

    def front(front_weights):
        coarse = leaf_front(ordered, *front_weights[:6])
        coarse_normed = rms_scale(coarse, front_weights[6])
        block_means = jnp.mean(coarse.reshape(ROOT_DEV, -1, coarse.shape[-1]), axis=1)
        return (coarse, coarse_normed, rms_scale(block_means, front_weights[6]))

    front_weights = (gain_leaf, w_qkv_leaf, w_out_leaf, w_pool1, w_pool2, w_pool3, gain_coarse)
    (coarse, coarse_normed, own_roots), pull_front = jax.vjp(front, front_weights)
    root_rows = lax.all_gather(own_roots, ("grp", "leaf"), axis=0, tiled=True)
    queries = matmul_high(coarse_normed, w_query)
    own_keyval = matmul_high(coarse_normed, w_keyval)
    group_keyval = lax.all_gather(own_keyval, "leaf", axis=0, tiled=True)
    root_keyval = matmul_high(root_rows, w_keyval)
    bottleneck, pull_attend = jax.vjp(attend, queries, group_keyval, root_keyval)
    output = coarse + matmul_high(bottleneck, w_out)
    grad_out = matmul_high(bottleneck.T, cotangent)
    d_bottleneck = matmul_high(cotangent, w_out.T)
    d_queries, d_group, d_rootkv = pull_attend(d_bottleneck)
    grad_query = matmul_high(coarse_normed.T, d_queries)
    d_normed = matmul_high(d_queries, w_query.T)
    grad_keyval = matmul_high(root_rows.T, d_rootkv)
    d_root_rows = matmul_high(d_rootkv, w_keyval.T)
    d_own_keyval = lax.psum_scatter(d_group, "leaf", scatter_dimension=0, tiled=True)
    grad_keyval = grad_keyval + matmul_high(coarse_normed.T, d_own_keyval)
    d_normed = d_normed + matmul_high(d_own_keyval, w_keyval.T)
    d_own_roots = lax.psum_scatter(d_root_rows, ("grp", "leaf"), scatter_dimension=0, tiled=True)
    front_grads = pull_front((cotangent, d_normed, d_own_roots))[0]
    totals = lax.psum(
        (
            front_grads[0],
            front_grads[1],
            front_grads[2],
            front_grads[3],
            front_grads[4],
            front_grads[5],
            front_grads[6],
            grad_query,
            grad_keyval,
            grad_out,
        ),
        ("grp", "leaf"),
    )
    return (
        output,
        totals[0],
        totals[1],
        totals[2],
        totals[3],
        totals[4],
        totals[5],
        totals[6],
        totals[7],
        totals[8],
        totals[9],
    )


def solution(mesh):
    placed = (
        P(("grp", "leaf"), None),
        P(("grp", "leaf"), None),
        P(),
        P(),
        P(),
        P(),
        P(),
        P(),
        P(),
        P(),
        P(),
        P(),
        P(("grp", "leaf"), None),
    )
    return jax.shard_map(
        shards,
        mesh=mesh,
        in_specs=placed,
        out_specs=(P(("grp", "leaf"), None), P(), P(), P(), P(), P(), P(), P(), P(), P(), P()),
        check_vma=False,
    )
```

profile of v0, /device:TPU:1, one launch (start us, length us, event | category | flops | bytes accessed | tf_op | source)
XLA Modules:
  0.0 820.9 jit_solution(17208830188989891000)
XLA Ops:
  8.9 5.1 gather_fusion
  15.9 2.6 convolution_bitcast_fusion
  20.0 3.4 fusion.31
  23.4 2.3 fusion.103
  25.8 1.9 convolution_bitcast_fusion.4
  28.9 1.8 convolution_add_fusion.1
  30.7 1.9 reshape.216
  32.6 2.6 fusion.42
  36.2 3.2 fusion.72
  44.0 2.2 fusion.107
  46.3 1.8 convolution_multiply_fusion.1
  49.1 304.0 %all-gather = f32[128,2,512]{2,1,0:T(2,128)} all-gather(f32[1,2,512]{2,1,0:T(2,128)S(1)} %multiply_bitcast_fusion), channel_id=1, replica_groups=mesh['grp'=4,'leaf'=32] {'grp','leaf'}, dimensions={0}, use_global_device_ids=true | all-gather | bytes 528384 | tf_op jit(solution)/shard_map/all_gather | solution.py:86
  353.1 2.2 reshape.243
  355.4 3.7 fusion.106
  360.1 2.1 copy.75
  362.2 2.0 copy.74
  365.7 2.7 fusion.105
  372.4 4.5 fusion.24
  377.0 3.0 fusion.100
  380.0 2.5 copy.72
  382.5 2.0 fusion.68
  386.7 2.5 copy.71
  389.2 2.2 multiply_reduce_fusion.1
  395.2 2.9 copy.92
  399.5 6.2 fusion.23
  405.6 148.8 %all-reduce.13.cloned.1.call-done = f32[256,512]{1,0:T(8,128)} async-done(((f32[256,512]{1,0:T(8,128)}), f32[256,512]{1,0:T(8,128)}) %all-reduce.13.cloned.1.call-update) | async-done | bytes 524304
  557.4 2.6 fusion.95
  561.4 2.4 fusion.50
  565.7 2.2 fusion.108
  567.9 2.0 fusion.111
  570.0 2.1 fusion.74
  572.0 3.6 multiply_reduce_fusion.4
  575.7 2.9 fusion.109
  579.3 3.1 fusion.93
  582.5 1.8 fusion.96
  584.3 1.9 fusion.98
  587.8 3.4 convolution_bitcast_fusion.2
  591.2 3.5 multiply_reduce_fusion
  594.7 2.6 fusion.14
  597.3 3.6 convolution_bitcast_fusion.1
  601.0 2.6 fusion.91
  603.6 4.3 fusion.110
  610.5 2.8 fusion.3
  613.3 3.4 convolution_add_fusion
  619.2 2.8 fusion.16
  622.0 83.8 %all-reduce.8 = (f32[128]{0:T(128)}, f32[512]{0:T(512)}) all-reduce(f32[128]{0:T(128)S(1)} %fusion.16, f32[512]{0:T(512)S(1)} %add_any.77), channel_id=1, replica_groups=mesh['grp'=4,'leaf'=32] {'grp','leaf'}, use_global_device_ids=true, to_apply=%region_18.19 | all-reduce | flops 640 | bytes 5120 | tf_op jit(solution)/shard_map/psum | solution.py:105
  705.8 94.1 %all-reduce.15.cloned.1.call-done = (f32[128,384]{1,0:T(8,128)}, f32[128,128]{1,0:T(8,128)}, f32[512,256]{1,0:T(8,128)}, f32[1024,384]{1,0:T(8,128)}, f32[1536,5...) async-done(((f32[128,384]{1,0:T(8,128)}, f32[128,128]{1,0:T(8,128)}, f32[512,256]{1,0:T(8,128)}, f32[1024,384]{1,0:T(8,128)}, ...) | async-done | bytes 9699344 | tf_op jit(solution)/shard_map/psum | solution.py:105
  803.1 2.0 copy.172
  (241 shorter events, 50.4 us)
Async XLA Ops:
  8.0 32.4 %copy-start = (f32[1536,512]{1,0:T(8,128)S(1)}, f32[1536,512]{1,0:T(8,128)}, u32[]{:S(2)}) copy-start(f32[1536,512]{1,0:T(8,128)} %param.20) | copy-start | bytes 9437188
  8.0 368.9 %all-gather.3.cloned.1.call-start = ((), (), s32[]{:S(2)}) async-start(), calls=%async_computation.1 | async-start | bytes 2162688 | tf_op jit(solution)/shard_map/all_gather | solution.py:89
  8.9 7.0 copy-start.45
  8.9 7.0 copy-start.76
  19.0 6.8 copy-start.30
  40.4 3.6 copy-start.41
  40.4 3.6 copy-start.52
  42.1 6.0 copy-start.83
  42.1 6.1 copy-start.21
  42.2 6.0 copy-start.72
  44.0 510.5 %all-reduce.13.cloned.1.call-start = ((), (), s32[]{:S(2)}) async-start(), calls=%async_computation.3 | async-start | bytes 1048576
  48.3 315.9 %copy-start.17 = (f32[16,16,32]{2,1,0:T(8,128)}, f32[16,16,32]{2,1,0:T(8,128)S(1)}, u32[]{:S(2)}) copy-start(f32[16,16,32]{2,1,0:T(8,128)S(1)} %mul.288) | copy-start | bytes 98308
  49.0 310.0 %copy-start.78 = (f32[2]{0:T(128)}, f32[2]{0:T(128)S(1)}, u32[]{:S(2)}) copy-start(f32[2]{0:T(128)S(1)} %get-tuple-element.33) | copy-start | bytes 28
  365.7 5.1 copy-start.18
  365.7 6.7 copy-start.3
  376.9 195.1 %reduce-scatter.4.cloned.1.call-start = ((), (), s32[]{:S(2)}) async-start(), calls=%async_computation.2 | async-start | bytes 2162688
  398.2 156.3 %copy-start.79 = (f32[2]{0:T(128)S(1)}, f32[2]{0:T(128)}, u32[]{:S(2)}) copy-start(f32[2]{0:T(128)} %copy-done.78) | copy-start | bytes 28
  398.2 157.8 %copy-start.82 = (f32[2]{0:T(128)S(1)}, f32[2]{0:T(128)}, u32[]{:S(2)}) copy-start(f32[2]{0:T(128)} %copy-done.81) | copy-start | bytes 28
  398.2 157.8 %copy-start.80 = (f32[2]{0:T(128)S(1)}, f32[2]{0:T(128)}, u32[]{:S(2)}) copy-start(f32[2]{0:T(128)} %get-tuple-element.32) | copy-start | bytes 28
  398.2 159.2 %copy-start.61 = (f32[16,16]{1,0:T(8,128)S(1)}, f32[16,16]{1,0:T(8,128)}, u32[]{:S(2)}) copy-start(f32[16,16]{1,0:T(8,128)} %copy-done.59) | copy-start | bytes 3076
  398.2 159.2 %copy-start.71 = (f32[16,16]{1,0:T(8,128)S(1)}, f32[16,16]{1,0:T(8,128)}, u32[]{:S(2)}) copy-start(f32[16,16]{1,0:T(8,128)} %copy-done.70) | copy-start | bytes 3076
  398.2 401.7 %all-reduce.15.cloned.1.call-start = ((), (), s32[]{:S(2)}) async-start(), calls=%async_computation.4 | async-start | bytes 19398656 | tf_op jit(solution)/shard_map/psum | solution.py:105
  399.5 160.5 %copy-start.63 = (f32[16,16]{1,0:T(8,128)S(1)}, f32[16,16]{1,0:T(8,128)}, u32[]{:S(2)}) copy-start(f32[16,16]{1,0:T(8,128)} %copy-done.62) | copy-start | bytes 3076
  554.5 5.5 copy-start.15
  554.5 5.5 copy-start.25
  561.4 4.3 copy-start.51
  561.4 6.5 copy-start.53
  563.9 6.1 copy-start.22
  563.9 6.1 copy-start.73
  565.7 9.9 %copy-start.49 = (f32[16,512]{1,0:T(8,128)}, f32[16,512]{1,0:T(8,128)S(1)}, u32[]{:S(2)}) copy-start(f32[16,512]{1,0:T(8,128)S(1)} %add.122) | copy-start | bytes 98308
  567.9 7.7 copy-start.84
  567.9 7.7 copy-start.54
  567.9 7.7 copy-start.74
  575.6 3.7 copy-start.40
  578.6 3.9 copy-start.12
  578.6 3.9 copy-start.23
  584.3 3.5 copy-start.9
  587.8 3.4 copy-start.31
  587.8 3.4 copy-start.69
  591.2 3.5 copy-start.36
  597.3 3.6 copy-start.27
  597.3 3.6 copy-start.44
  597.3 6.2 copy-start.48
  603.6 4.3 copy-start.14
  603.6 4.3 copy-start.32
  609.4 4.0 copy-start.7
  609.4 4.0 copy-start.55
  799.9 5.2 copy-start.37
  (41 other events, 73.5 us)
Sparse Core Ops, SparseCore 0:
  44.1 136.1 all-gather.2
  398.3 170.3 reduce-scatter.3
Sparse Core Ops, SparseCore 1:
  377.0 177.5 all-reduce.12
  616.9 183.0 all-reduce.14
where the time goes:
time: 827 us; the launch traced here: 821 us
  blocking collectives  388 us (47%)
  waiting for transfers between devices  243 us (29%)
  matrix products  107 us (13%)
  local copies, waits for them, and re-layouts  51.1 us (6%)
  between operations  16.8 us (2%)
  other arithmetic  14.7 us (2%)
    all_gather x1, blocking collectives, shards(): root_rows = lax.all_gather(own_roots, ('grp', 'leaf'), axis=0, tiled=True)  304 us
    unnamed x6, waiting for transfers between devices  149 us
    psum x1, waiting for transfers between devices, shards(): lax.psum((front_grads[0], front_grads[1], front_grads[2], front_grads[3],...  94.1 us
    psum x1, blocking collectives, shards(): lax.psum((front_grads[0], front_grads[1], front_grads[2], front_grads[3],...  83.8 us
    dot_general x27, matrix products, matmul_high(): jnp.dot(left, right, precision=MATMUL_ACCURACY, preferred_element_type=jn...  70.5 us
    unnamed x181, local copies, waits for them, and re-layouts  25.2 us
  transfers between devices with their start and end apart: 4, of which 2 were waited for; matrix products, arithmetic and copies ran while one was open for 9% of the time, Pallas kernels for 0%

commit v1 on v0

v1 whole, which is shorter than its diff:
```python
import jax
import jax.numpy as jnp
from jax import lax
from jax.sharding import Mesh
from jax.sharding import PartitionSpec as P

HEAD = 32
BALL = 128
ROOT_DEV = 2
GRP = ("zh", "co")
LEAF = ("zl", "y", "x")
ALL = GRP + LEAF
N_LEAF = 32
N_GRP = 4
HEADS = 16

PREC = lax.Precision.HIGHEST


def mm(left, right):
    return jnp.dot(left, right, precision=PREC, preferred_element_type=jnp.float32)


def mm_t(left, right):
    return lax.dot_general(
        left, right, (((1,), (1,)), ((), ())), precision=PREC, preferred_element_type=jnp.float32
    )


def t_mm(left, right):
    return lax.dot_general(
        left, right, (((0,), (0,)), ((), ())), precision=PREC, preferred_element_type=jnp.float32
    )


def rms_scale(values, gain):
    return values * lax.rsqrt(jnp.mean(values * values, axis=-1, keepdims=True) + 1e-06) * gain


def leaf_front(ordered, gain_leaf, w_qkv_leaf, w_out_leaf, w_pool1, w_pool2, w_pool3):
    row_count, feature_width = ordered.shape
    head_count = feature_width // HEAD
    leaf_normed = rms_scale(ordered, gain_leaf)
    packed = mm(leaf_normed, w_qkv_leaf).reshape(row_count // BALL, BALL, 3, head_count, HEAD)
    queries = packed[:, :, 0] * HEAD ** (-0.5)
    scores = jnp.einsum("bihd,bjhd->bhij", queries, packed[:, :, 1], precision=PREC)
    weights = jax.nn.softmax(scores, axis=-1)
    attended = jnp.einsum("bhij,bjhd->bihd", weights, packed[:, :, 2], precision=PREC)
    leaf_mixed = ordered + mm(attended.reshape(row_count, feature_width), w_out_leaf)
    level_one = jax.nn.silu(mm(leaf_mixed.reshape(row_count // 4, -1), w_pool1))
    level_two = jax.nn.silu(mm(level_one.reshape(row_count // 16, -1), w_pool2))
    return mm(level_two.reshape(row_count // 64, -1), w_pool3)


def part(queries, keys, values, d_out):
    scores = mm_t(queries, keys) * HEAD ** (-0.5)
    weights = jax.nn.softmax(scores, axis=-1)
    out = mm(weights, values)
    d_values = t_mm(weights, d_out)
    d_weights = mm_t(d_out, values)
    d_scores = weights * (d_weights - jnp.sum(weights * d_weights, axis=-1, keepdims=True))
    d_scores = d_scores * HEAD ** (-0.5)
    return out, mm(d_scores, keys), t_mm(d_scores, queries), d_values


def heads_out(rows):
    return rows.reshape(rows.shape[0], HEADS, HEAD).transpose(1, 0, 2)


def heads_in(blocks):
    return blocks.transpose(1, 0, 2).reshape(blocks.shape[1], HEADS * HEAD)


def shards(
    features,
    tree_order,
    gain_leaf,
    w_qkv_leaf,
    w_out_leaf,
    w_pool1,
    w_pool2,
    w_pool3,
    gain_coarse,
    w_query,
    w_keyval,
    w_out,
    cotangent,
):
    half = lax.axis_index("x") % 2
    ordered = features[tree_order[0]]

    def front(front_weights):
        coarse = leaf_front(ordered, *front_weights[:6])
        coarse_normed = rms_scale(coarse, front_weights[6])
        block_means = jnp.mean(coarse.reshape(ROOT_DEV, -1, coarse.shape[-1]), axis=1)
        rows = jnp.concatenate([coarse_normed, rms_scale(block_means, front_weights[6])], axis=0)
        return coarse, rows

    front_weights = (gain_leaf, w_qkv_leaf, w_out_leaf, w_pool1, w_pool2, w_pool3, gain_coarse)
    (coarse, rows), pull_front = jax.vjp(front, front_weights)
    d_bottleneck = mm_t(cotangent, w_out)
    keyval = mm(rows, w_keyval)
    queries = mm(rows[:16], w_query)
    roots = lax.all_gather(keyval[16:].reshape(16, 128), GRP, axis=0, tiled=True).reshape(8, 1024)
    main = jnp.concatenate(
        [
            heads_out(queries),
            heads_out(keyval[:16, :512]),
            heads_out(keyval[:16, 512:]),
            heads_out(d_bottleneck),
        ],
        axis=-1,
    )
    side = jnp.concatenate([heads_out(roots[:, :512]), heads_out(roots[:, 512:])], axis=-1)
    side = jnp.concatenate([side, jnp.zeros_like(side)], axis=-1)
    message = jnp.concatenate([main, side], axis=1)
    message = jnp.broadcast_to(message[:, None], (HEADS, 2, 24, 128)).reshape(N_LEAF, 24, 128)
    got = lax.all_to_all(message, LEAF, 0, 0, tiled=True)
    mine = lax.dynamic_slice(got, (0, half * 8, 0), (N_LEAF, 8, 128)).reshape(256, 128)
    every = got[:, :16].reshape(512, 128)
    away = got[:, 16:].reshape(256, 128)
    q, d_o = mine[:, :32], mine[:, 96:]
    out_a, dq_a, dk_a, dv_a = part(q, every[:, 32:64], every[:, 64:96], d_o)
    out_b, dq_b, dk_b, dv_b = part(q, away[:, :32], away[:, 32:64], d_o)
    front_half = jnp.concatenate([out_a + out_b, dq_a + dq_b], axis=-1).reshape(N_LEAF, 8, 64)
    front_half = lax.dynamic_update_slice(
        jnp.zeros((N_LEAF, 16, 64), jnp.float32), front_half, (0, half * 8, 0)
    )
    back_half = jnp.concatenate([dk_a, dv_a], axis=-1).reshape(N_LEAF, 16, 64)
    side = jnp.concatenate([dk_b, dv_b], axis=-1).reshape(N_LEAF, 8, 64)
    side = jnp.concatenate([side, jnp.zeros_like(side)], axis=-1)
    message = jnp.concatenate([jnp.concatenate([front_half, back_half], axis=-1), side], axis=1)
    got = lax.all_to_all(message, LEAF, 0, 0, tiled=True)
    got = got.reshape(HEADS, 2, 24, 128)
    got = got[:, 0] + got[:, 1]
    bottleneck = heads_in(got[:, :16, :32])
    d_queries = heads_in(got[:, :16, 32:64])
    d_keyval = jnp.concatenate([heads_in(got[:, :16, 64:96]), heads_in(got[:, :16, 96:])], axis=-1)
    d_roots = jnp.concatenate([heads_in(got[:, 16:, :32]), heads_in(got[:, 16:, 32:64])], axis=-1)
    d_roots = lax.all_to_all(d_roots.reshape(64, 128), GRP, 0, 0, tiled=True)
    d_roots = jnp.sum(d_roots.reshape(N_GRP, 2, 1024), axis=0)
    d_keyval = jnp.concatenate([d_keyval, d_roots], axis=0)
    output = coarse + mm(bottleneck, w_out)
    grad_out = t_mm(bottleneck, cotangent)
    grad_query = t_mm(rows[:16], d_queries)
    grad_keyval = t_mm(rows, d_keyval)
    d_rows = mm_t(d_keyval, w_keyval)
    d_rows = d_rows + jnp.pad(mm_t(d_queries, w_query), ((0, 2), (0, 0)))
    grads = pull_front((cotangent, d_rows))[0]
    gains = jnp.concatenate([grads[0], grads[6], jnp.zeros((384,), jnp.float32)]).reshape(8, 128)
    low = jnp.concatenate([grads[2], gains], axis=0)
    totals = lax.psum(
        (grads[1], low, grads[3], grads[4], grads[5], grad_query, grad_keyval, grad_out), ALL
    )
    gains = totals[1][128:].reshape(1024)
    return (
        output,
        gains[:128],
        totals[0],
        totals[1][:128],
        totals[2],
        totals[3],
        totals[4],
        gains[128:640],
        totals[5],
        totals[6],
        totals[7],
    )


def solution(mesh):
    fine = Mesh(mesh.devices.reshape(2, 2, 2, 4, 4), ALL)
    cut = P(ALL, None)
    return jax.shard_map(
        shards,
        mesh=fine,
        in_specs=(cut, cut) + (P(),) * 10 + (cut,),
        out_specs=(cut,) + (P(),) * 10,
        check_vma=False,
    )
```

time: 827 us -> 389 us (0.47)
  blocking collectives: 388 us -> 8.43 us
  waiting for transfers between devices: 243 us -> 178 us
  matrix products: 107 us -> 84 us
  starting transfers between devices: 0.34 us -> 20.7 us
    all_gather x1, blocking collectives: 304 us -> 8.43 us  [shards(): lax.all_gather(keyval[16:].reshape(16, 128), GRP, axis=0, tiled=True)]
    unnamed x6 -> x1, waiting for transfers between devices: 149 us -> 0.02 us
    psum x1 -> x0, blocking collectives: 83.8 us -> none  [shards(): lax.psum((front_grads[0], front_grads[1], front_grads[2], front_grads[3],...]
    psum x1, waiting for transfers between devices: 94.1 us -> 161 us  [shards(): lax.psum((grads[1], low, grads[3], grads[4], grads[5], grad_query, grad_k...]
    dot_general x45 -> x40, matrix products: 107 us -> 84 us  [the longest x20 42.9 us: mm(): jnp.dot(left, right, precision=PREC, preferred_element_type=jnp.float32)]
    all_to_all x0 -> x3, starting transfers between devices: none -> 20.5 us  [the longest x2 12.9 us: shards(): got = lax.all_to_all(message, LEAF, 0, 0, tiled=True)]
    all_to_all x0 -> x3, waiting for transfers between devices: none -> 17.4 us  [the longest x2 16 us: shards(): got = lax.all_to_all(message, LEAF, 0, 0, tiled=True)]
    reshape x7 -> x21, local copies, waits for them, and re-layouts: 4.89 us -> 14.1 us  [the longest x6 5.28 us: heads_in(): return blocks.transpose(1, 0, 2).reshape(blocks.shape[1], HEADS * HEAD)]
  transfers between devices with their start and end apart: 4 -> 4, of which waited for: 2 -> 4; matrix products, arithmetic and copies ran while one was open for 9% -> 2% of each run, Pallas kernels for 0% -> 0%
where the time goes in v1:
time: 389 us; the launch traced here: 383 us
  waiting for transfers between devices  178 us (46%)
  matrix products  84 us (22%)
  local copies, waits for them, and re-layouts  50.1 us (13%)
  other arithmetic  21.1 us (5%)
  starting transfers between devices  20.7 us (5%)
  between operations  15.5 us (4%)
  blocking collectives  8.43 us (2%)
  Pallas kernels  4.86 us (1%)
    psum x1, waiting for transfers between devices, shards(): lax.psum((grads[1], low, grads[3], grads[4], grads[5], grad_query, grad_k...  161 us
    dot_general x20, matrix products, mm(): jnp.dot(left, right, precision=PREC, preferred_element_type=jnp.float32)  42.9 us
    unnamed x156, local copies, waits for them, and re-layouts  16.6 us
    all_to_all x2, waiting for transfers between devices, shards(): got = lax.all_to_all(message, LEAF, 0, 0, tiled=True)  16 us
    all_to_all x2, starting transfers between devices, shards(): got = lax.all_to_all(message, LEAF, 0, 0, tiled=True)  12.9 us
    dot_general x7, matrix products, t_mm(): lax.dot_general(left, right, (((0,), (0,)), ((), ())), precision=PREC, pr...  11.9 us
    dot_general x7, matrix products, mm_t(): lax.dot_general(left, right, (((1,), (1,)), ((), ())), precision=PREC, pr...  11 us
    dot_general x3, matrix products, leaf_front(): jnp.einsum('bihd,bjhd->bhij', queries, packed[:, :, 1], precision=PREC)  9.18 us
  transfers between devices with their start and end apart: 4, of which 4 were waited for; matrix products, arithmetic and copies ran while one was open for 2% of the time, Pallas kernels for 0%

profile of v1, /device:TPU:1, one launch (start us, length us, event | category | flops | bytes accessed | tf_op | source)
XLA Modules:
  0.0 382.8 jit_solution(6321316320681676489)
XLA Ops:
  8.1 5.1 %gather_fusion = f32[1024,128]{1,0:T(8,128)} fusion(f32[1024,128]{1,0:T(8,128)} %param.13, s32[1024]{0:T(1024)S(1)} %broadcast_clamp_fusion), kind=kCustom, calls=%fused_computation | custom fusion | bytes 1052672 | tf_op jit(solution)/shard_map/gather | solution.py:90
  15.1 2.6 convolution_bitcast_fusion
  19.1 3.4 fusion.20
  22.5 2.3 fusion.101
  24.9 1.9 convolution_bitcast_fusion.4
  27.9 1.8 convolution_add_fusion
  29.7 1.9 reshape.241
  31.6 2.6 fusion.33
  35.3 3.2 fusion.65
  39.4 1.6 bitcast_reduce_fusion
  44.9 1.8 fusion.104
  46.8 8.4 %all_gather.3 = f32[64,128]{1,0:T(8,128)S(1)} all-gather(f32[16,128]{1,0:T(8,128)S(1)} %reshape.249), channel_id=1, replica_groups=mesh['zh'=2,'co'=2,'zl'=2,'y'=4,'x'=4] {'zh','co'}, dimensions={0}, use_global_device_ids=true | all-gather | bytes 40960 | tf_op jit(solution)/shard_map/all_gather | solution.py:104
  61.2 8.4 %all-to-all-start = ((f32[32,24,128]{2,1,0:T(8,128)}), f32[32,24,128]{2,1,0:T(8,128)S(1)}, u32[]{:S(2)}, u32[]{:S(2)}) async-start(f32[32,24,128]{2,1,0:T(8,128)} %bitcast.159), calls=%async_computation | async-start | bytes 786432 | tf_op jit(solution)/shard_map/all_to_all | solution.py:118
  69.7 8.9 %all-to-all-done = f32[32,24,128]{2,1,0:T(8,128)S(1)} async-done(((f32[32,24,128]{2,1,0:T(8,128)}), f32[32,24,128]{2,1,0:T(8,128)S(1)}, u32[]{:S(2)}, u32[]{:S(2)}) %all-to-all-start) | async-done | bytes 393248 | tf_op jit(solution)/shard_map/all_to_all | solution.py:118
  85.9 2.1 multiply_reduce_fusion.1
  87.9 2.2 online-softmax.1
  90.9 2.6 online-softmax
  93.6 2.6 fusion.59
  96.2 2.3 convolution_add_fusion.3
  98.4 1.5 copy.68
  99.9 1.5 pad_maximum_fusion
  104.5 1.8 select_maximum_fusion
  106.3 4.5 %all-to-all-start.1 = ((f32[32,24,128]{2,1,0:T(8,128)}), f32[32,24,128]{2,1,0:T(8,128)S(1)}, u32[]{:S(2)}, u32[]{:S(2)}) async-start(f32[32,24,128]{2,1,0:T(8,128)} %select_maximum_fusion), calls=%async_computation.1 | async-start | bytes 786432 | tf_op jit(solution)/shard_map/all_to_all | solution.py:133
  112.1 7.1 %all-to-all-done.1 = f32[32,24,128]{2,1,0:T(8,128)S(1)} async-done(((f32[32,24,128]{2,1,0:T(8,128)}), f32[32,24,128]{2,1,0:T(8,128)S(1)}, u32[]{:S(2)}, u32[]{:S(2)}) %all-to-all-start.1) | async-done | bytes 393248 | tf_op jit(solution)/shard_map/all_to_all | solution.py:133
  121.9 2.8 fusion.106
  124.7 2.0 fusion.109
  126.7 1.5 reshape.264
  128.2 1.5 reshape.265
  131.1 7.7 %all-to-all-start.2 = ((f32[4,16,128]{2,1,0:T(8,128)}), f32[4,16,128]{2,1,0:T(8,128)}, u32[]{:S(2)}, u32[]{:S(2)}) async-start(f32[4,16,128]{2,1,0:T(8,128)} %all_to_all.14), calls=%async_computation.2 | async-start | bytes 65536 | tf_op jit(solution)/shard_map/all_to_all | solution.py:140
  139.9 2.0 fusion.110
  144.3 3.4 convolution_add_fusion.1
  153.7 2.7 fusion.107
  156.4 3.1 fusion.85
  159.7 1.8 fusion.87
  161.5 1.9 fusion.89
  164.9 3.4 convolution_bitcast_fusion.2
  168.3 3.7 multiply_reduce_fusion
  172.1 2.2 fusion.10
  174.3 3.6 convolution_bitcast_fusion.1
  179.2 2.8 fusion.11
  182.0 3.0 fusion.1
  185.0 2.6 fusion.83
  187.6 3.2 fusion.66
  190.8 4.3 %fusion.108 = f32[1536,512]{1,0:T(8,128)} fusion(f32[16,1536]{1,0:T(8,128)S(1)} %copy-done.39, f32[16,512]{1,0:T(8,128)S(1)} %copy-done.48), kind=kOutput, calls=%fused_computation.169 | convolution fusion | flops 150994944 | bytes 3276800 | tf_op jit(solution)/shard_map/transpose(jvp())/dot_general | solution.py:21
  199.0 160.7 %all-reduce.8.cloned.1.call-done = (f32[136,128]{1,0:T(8,128)}, f32[128,384]{1,0:T(8,128)}, f32[512,256]{1,0:T(8,128)}, f32[1024,384]{1,0:T(8,128)}, f32[1536,51...) async-done(((f32[136,128]{1,0:T(8,128)}, f32[128,384]{1,0:T(8,128)}, f32[512,256]{1,0:T(8,128)}, f32[1024,384]{1,0:T(8,128)}, ...) | async-done | bytes 9703440 | tf_op jit(solution)/shard_map/psum | solution.py:152
  363.7 1.6 copy.139
  365.3 2.0 copy.140
  368.5 1.7 copy.142
  (243 shorter events, 59.9 us)
Async XLA Ops:
  7.2 32.2 %copy-start = (f32[1536,512]{1,0:T(8,128)S(1)}, f32[1536,512]{1,0:T(8,128)}, u32[]{:S(2)}) copy-start(f32[1536,512]{1,0:T(8,128)} %param.20) | copy-start | bytes 9437188
  8.0 7.0 %copy-start.42 = (f32[128,384]{1,0:T(8,128)S(1)}, f32[128,384]{1,0:T(8,128)}, u32[]{:S(2)}) copy-start(f32[128,384]{1,0:T(8,128)} %param.16) | copy-start | bytes 589828
  8.1 7.0 %copy-start.67 = (f32[128]{0:T(128)S(1)}, f32[128]{0:T(128)}, u32[]{:S(2)}) copy-start(f32[128]{0:T(128)} %param.15) | copy-start | bytes 1540
  18.2 6.7 %copy-start.24 = (f32[8,128,1,4,32]{1,0,4,3,2:T(8,128)}, f32[8,128,1,4,32]{1,0,4,3,2:T(8,128)S(1)}, u32[]{:S(2)}) copy-start(f32[8,128,1,4,32]{1,0,4,3,2:T(8,128)S(1)} %get-tuple-element.23) | copy-start | bytes 1572868
  24.8 3.1 copy-start.2
  24.8 3.1 copy-start.54
  35.2 5.8 %copy-start.19 = (f32[64,1024]{1,0:T(8,128)}, f32[64,1024]{1,0:T(8,128)S(1)}, u32[]{:S(2)}) copy-start(f32[64,1024]{1,0:T(8,128)S(1)} %reshape.242) | copy-start | bytes 786436
  38.5 3.4 copy-start.56
  39.4 3.8 copy-start.38
  39.4 4.4 %copy-start.12 = (f32[512,512]{1,0:T(8,128)S(1)}, f32[512,512]{1,0:T(8,128)}, u32[]{:S(2)}) copy-start(f32[512,512]{1,0:T(8,128)} %param.24) | copy-start | bytes 3145732
  39.4 4.4 %copy-start.51 = (f32[16,512]{1,0:T(8,128)S(1)}, f32[16,512]{1,0:T(8,128)}, u32[]{:S(2)}) copy-start(f32[16,512]{1,0:T(8,128)} %param.25) | copy-start | bytes 98308
  41.2 3.6 copy-start.71
  41.3 5.4 %copy-start.66 = (f32[16]{0:T(128)}, f32[16]{0:T(128)S(1)}, u32[]{:S(2)}) copy-start(f32[16]{0:T(128)S(1)} %fusion.73) | copy-start | bytes 196
  42.0 4.8 %copy-start.62 = (f32[2,512]{1,0:T(2,128)}, f32[2,512]{1,0:T(2,128)S(1)}, u32[]{:S(2)}) copy-start(f32[2,512]{1,0:T(2,128)S(1)} %multiply_multiply_fusion.7) | copy-start | bytes 12292
  42.0 4.7 %copy-start.40 = (f32[16,512]{1,0:T(8,128)}, f32[16,512]{1,0:T(8,128)S(1)}, u32[]{:S(2)}) copy-start(f32[16,512]{1,0:T(8,128)S(1)} %multiply_multiply_fusion.4) | copy-start | bytes 98308
  61.2 17.3 %all-to-all-start = ((f32[32,24,128]{2,1,0:T(8,128)}), f32[32,24,128]{2,1,0:T(8,128)S(1)}, u32[]{:S(2)}, u32[]{:S(2)}) async-start(f32[32,24,128]{2,1,0:T(8,128)} %bitcast.159), calls=%async_computation | async-start | bytes 786432 | tf_op jit(solution)/shard_map/all_to_all | solution.py:118
  78.6 7.3 %copy-start.34 = (f32[256,128]{1,0:T(8,128)}, f32[256,128]{1,0:T(8,128)S(1)}, u32[]{:S(2)}) copy-start(f32[256,128]{1,0:T(8,128)S(1)} %get-tuple-element.29) | copy-start | bytes 393220
  82.8 3.1 copy-start.16
  87.9 8.2 %copy-start.17 = (f32[32,16,128]{2,1,0:T(8,128)S(1)}, f32[32,16,128]{2,1,0:T(8,128)}, u32[]{:S(2)}) copy-start(f32[32,16,128]{2,1,0:T(8,128)} %copy-done.16) | copy-start | bytes 786436
  96.2 6.3 %copy-start.44 = (f32[256,32]{1,0:T(8,128)S(1)}, f32[256,32]{1,0:T(8,128)}, u32[]{:S(2)}) copy-start(f32[256,32]{1,0:T(8,128)} %online-softmax) | copy-start | bytes 98308
  106.3 12.9 %all-to-all-start.1 = ((f32[32,24,128]{2,1,0:T(8,128)}), f32[32,24,128]{2,1,0:T(8,128)S(1)}, u32[]{:S(2)}, u32[]{:S(2)}) async-start(f32[32,24,128]{2,1,0:T(8,128)} %select_maximum_fusion), calls=%async_computation.1 | async-start | bytes 786432 | tf_op jit(solution)/shard_map/all_to_all | solution.py:133
  119.2 5.4 %copy-start.41 = (f32[16,512]{1,0:T(8,128)S(1)}, f32[16,512]{1,0:T(8,128)}, u32[]{:S(2)}) copy-start(f32[16,512]{1,0:T(8,128)} %copy-done.40) | copy-start | bytes 98308
  119.3 20.6 %copy-start.52 = (f32[16,512]{1,0:T(8,128)S(1)}, f32[16,512]{1,0:T(8,128)}, u32[]{:S(2)}) copy-start(f32[16,512]{1,0:T(8,128)} %param.25) | copy-start | bytes 98308
  128.2 20.8 %copy-start.33 = (f32[16,512]{1,0:T(8,128)S(1)}, f32[16,512]{1,0:T(8,128)}, u32[]{:S(2)}) copy-start(f32[16,512]{1,0:T(8,128)} %copy-done.32) | copy-start | bytes 98308
  131.1 12.4 %all-to-all-start.2 = ((f32[4,16,128]{2,1,0:T(8,128)}), f32[4,16,128]{2,1,0:T(8,128)}, u32[]{:S(2)}, u32[]{:S(2)}) async-start(f32[4,16,128]{2,1,0:T(8,128)} %all_to_all.14), calls=%async_computation.2 | async-start | bytes 65536 | tf_op jit(solution)/shard_map/all_to_all | solution.py:140
  138.7 221.0 %all-reduce.8.cloned.1.call-start = ((), (), s32[]{:S(2)}) async-start(), calls=%async_computation.3 | async-start | bytes 19406848 | tf_op jit(solution)/shard_map/psum | solution.py:152
  142.1 11.0 %copy-start.45 = (f32[16,512]{1,0:T(8,128)}, f32[16,512]{1,0:T(8,128)S(1)}, u32[]{:S(2)}) copy-start(f32[16,512]{1,0:T(8,128)S(1)} %reshape.263) | copy-start | bytes 98308
  142.1 10.3 %copy-start.53 = (f32[16,512]{1,0:T(8,128)S(1)}, f32[16,512]{1,0:T(8,128)}, u32[]{:S(2)}) copy-start(f32[16,512]{1,0:T(8,128)} %param.25) | copy-start | bytes 98308
  147.7 8.7 %copy-start.37 = (f32[64,384]{1,0:T(8,128)S(1)}, f32[64,384]{1,0:T(8,128)}, u32[]{:S(2)}) copy-start(f32[64,384]{1,0:T(8,128)} %get-tuple-element.47) | copy-start | bytes 294916
  156.3 3.3 copy-start.7
  156.3 3.3 copy-start.18
  161.5 3.4 copy-start.6
  161.5 3.4 copy-start.60
  164.9 3.4 copy-start.25
  164.9 3.4 copy-start.61
  168.3 3.8 copy-start.30
  178.0 3.9 %copy-start.68 = (f32[128]{0:T(128)S(1)}, f32[128]{0:T(128)}, u32[]{:S(2)}) copy-start(f32[128]{0:T(128)} %param.15) | copy-start | bytes 1540
  179.2 5.8 %copy-start.20 = (f32[64,1024]{1,0:T(8,128)S(1)}, f32[64,1024]{1,0:T(8,128)}, u32[]{:S(2)}) copy-start(f32[64,1024]{1,0:T(8,128)} %copy-done.19) | copy-start | bytes 786436
  182.0 5.7 %copy-start.46 = (f32[16,512]{1,0:T(8,128)S(1)}, f32[16,512]{1,0:T(8,128)}, u32[]{:S(2)}) copy-start(f32[16,512]{1,0:T(8,128)} %copy-done.45) | copy-start | bytes 98308
  182.0 5.7 %copy-start.63 = (f32[2,512]{1,0:T(2,128)S(1)}, f32[2,512]{1,0:T(2,128)}, u32[]{:S(2)}) copy-start(f32[2,512]{1,0:T(2,128)} %copy-done.62) | copy-start | bytes 12292
  185.0 5.8 %copy-start.39 = (f32[16,1536]{1,0:T(8,128)S(1)}, f32[16,1536]{1,0:T(8,128)}, u32[]{:S(2)}) copy-start(f32[16,1536]{1,0:T(8,128)} %copy-done.38) | copy-start | bytes 294916
  185.0 5.8 %copy-start.48 = (f32[16,512]{1,0:T(8,128)S(1)}, f32[16,512]{1,0:T(8,128)}, u32[]{:S(2)}) copy-start(f32[16,512]{1,0:T(8,128)} %copy-done.47) | copy-start | bytes 98308
  190.8 4.4 %copy-start.9 = (f32[8,128,4,32]{1,0,3,2:T(8,128)S(1)}, f32[8,128,4,32]{1,0,3,2:T(8,128)}, u32[]{:S(2)}) copy-start(f32[8,128,4,32]{1,0,3,2:T(8,128)} %copy-done.8) | copy-start | bytes 1572868
  190.8 4.4 %copy-start.26 = (f32[1024,128]{1,0:T(8,128)S(1)}, f32[1024,128]{1,0:T(8,128)}, u32[]{:S(2)}) copy-start(f32[1024,128]{1,0:T(8,128)} %reshape.270) | copy-start | bytes 1572868
  190.8 5.0 %copy-start.64 = (f32[512]{0:T(512)S(1)}, f32[512]{0:T(512)}, u32[]{:S(2)}) copy-start(f32[512]{0:T(512)} %get-tuple-element.12) | copy-start | bytes 6148
  190.8 5.0 %copy-start.65 = (f32[512]{0:T(512)S(1)}, f32[512]{0:T(512)}, u32[]{:S(2)}) copy-start(f32[512]{0:T(512)} %get-tuple-element.14) | copy-start | bytes 6148
  359.7 7.7 %copy-start.31 = (f32[1024,384]{1,0:T(8,128)S(1)}, f32[1024,384]{1,0:T(8,128)}, u32[]{:S(2)}) copy-start(f32[1024,384]{1,0:T(8,128)} %get-tuple-element.65) | copy-start | bytes 4718596
  365.3 3.2 copy-start.14
  (30 other events, 53.0 us)
Sparse Core Ops, SparseCore 0:
  196.7 162.9 all-reduce.7

commit v2 on v1

v2 whole, which is shorter than its diff:
```python
import jax
import jax.numpy as jnp
from jax import lax
from jax.experimental import pallas as pl
from jax.experimental.pallas import tpu as pltpu
from jax.sharding import Mesh
from jax.sharding import PartitionSpec as P

GRP = ("zh", "co")
LEAF = ("zl", "y", "x")
ALL = GRP + LEAF
N_LEAF = 32
HEADS = 16
SCALE = 32 ** (-0.5)
F32 = jnp.float32


def split(value):
    high = value.astype(jnp.bfloat16)
    return high, (value - high.astype(F32)).astype(jnp.bfloat16)


def dot3(left, right, dims):
    left_high, left_low = split(left)
    right_high, right_low = split(right)
    go = lambda a, b: lax.dot_general(a, b, (dims, ((), ())), preferred_element_type=F32)
    return go(left_high, right_high) + (go(left_high, right_low) + go(left_low, right_high))


def mm(left, right):
    return dot3(left, right, ((1,), (0,)))


def mm_t(left, right):
    return dot3(left, right, ((1,), (1,)))


def t_mm(left, right):
    return dot3(left, right, ((0,), (0,)))


def full(left, right, dims):
    return lax.dot_general(
        left, right, (dims, ((), ())), precision=lax.Precision.HIGHEST, preferred_element_type=F32
    )


def mm6(left, right):
    return full(left, right, ((1,), (0,)))


def mm6_t(left, right):
    return full(left, right, ((1,), (1,)))


def t_mm6(left, right):
    return full(left, right, ((0,), (0,)))


def lanes(at):
    lane = lax.broadcasted_iota(jnp.int32, (1, 128), 1)
    return ((lane >= 32 * at) & (lane < 32 * at + 32)).astype(F32)


def turn(value, by):
    by = by % 128
    return value if by == 0 else pltpu.roll(value, by, 1)


def inverse_rms(values):
    return lax.rsqrt(jnp.mean(values * values, axis=-1, keepdims=True) + 1e-06)


def sigmoid(pre):
    return 1.0 / (1.0 + jnp.exp(-pre))


def softmax(scores):
    weights = jnp.exp(scores - jnp.max(scores, axis=-1, keepdims=True))
    return weights / jnp.sum(weights, axis=-1, keepdims=True)


def four(value):
    return jnp.concatenate([value * lanes(h) for h in range(4)], axis=0)


def slot_one(rows, at):
    return rows.reshape(8, 4, 32, rows.shape[-1])[:, at].reshape(256, rows.shape[-1])


def slot_two(rows, at):
    return rows.reshape(8, 4, 8, rows.shape[-1])[:, at].reshape(64, rows.shape[-1])


def stride_get(ref, at, stride):
    blocks = [ref[j, pl.ds(at, 8, stride=stride), :] for j in range(ref.shape[0])]
    return jnp.concatenate(blocks, axis=1)


def stride_put(ref, at, stride, value):
    for j in range(ref.shape[0]):
        ref[j, pl.ds(at, 8, stride=stride), :] = value[:, 128 * j : 128 * j + 128]


def put_blocks(ref, value):
    for j in range(ref.shape[0]):
        ref[j] = value[:, 128 * j : 128 * j + 128]


def get_blocks(ref):
    return jnp.concatenate([ref[j] for j in range(ref.shape[0])], axis=1)


def slot_three(ref, at):
    return jnp.concatenate([stride_get(ref, 2 * at + a, 8) for a in range(2)], axis=0)


def forward_kernel(
    order, features, gain_leaf, w_qkv, w_out_leaf, w_one, w_two, w_three, gain_coarse, w_query,
    w_keyval, w_out, cotangent,
    unit, packed, weights, attended, mixed, pre_one, pre_two, two, coarse, rows, message, roots,
    ordered, natural,
):
    def fetch(step, carry):
        ball, rest = step // 16, step % 16
        base = ball * 128 + (rest % 4) * 4 + rest // 4
        for d2 in range(4):
            for a in range(2):
                source = order[0, base + 64 * a + 16 * d2]
                ordered[pl.ds(step * 8 + 2 * d2 + a, 1), :] = features[pl.ds(source, 1), :]
        return carry

    lax.fori_loop(0, 128, fetch, 0)
    unit[...] = ordered[...] * inverse_rms(ordered[...])
    packed[...] = mm6(unit[...] * gain_leaf[...], w_qkv[...])

    def ball(step, carry):
        at = pl.ds(step * 128, 128)
        values = packed[at, 256:]
        scores = mm6_t(four(packed[at, :128] * SCALE), packed[at, 128:256])
        probs = softmax(scores)
        weights[pl.ds(step * 512, 512), :] = probs
        wide = jnp.concatenate([probs[128 * h : 128 * h + 128] for h in range(4)], axis=1)
        attended[at, :] = mm6(wide, four(values))
        return carry

    lax.fori_loop(0, 8, ball, 0)
    joined = ordered[...] + mm6(attended[...], w_out_leaf[...])
    mixed[...] = joined
    pre = sum(mm6(slot_one(joined, d), w_one[128 * d : 128 * d + 128, :]) for d in range(4))
    pre_one[...] = pre
    one = pre * sigmoid(pre)
    pre = sum(mm6(slot_two(one, d), w_two[256 * d : 256 * d + 256, :]) for d in range(4))
    pre_two[...] = pre
    put_blocks(two, pre * sigmoid(pre))
    top = sum(mm6(slot_three(two, d), w_three[384 * d : 384 * d + 384, :]) for d in range(4))
    for a in range(2):
        stride_put(natural, a, 2, top[8 * a : 8 * a + 8])
    top = get_blocks(natural)
    coarse[...] = top
    means = jnp.concatenate(
        [jnp.mean(top[8 * r : 8 * r + 8], axis=0, keepdims=True) for r in range(2)]
        + [jnp.zeros((6, 512), F32)],
        axis=0,
    )
    normed = jnp.concatenate([top * inverse_rms(top), means * inverse_rms(means)], axis=0)
    normed = normed * gain_coarse[...]
    rows[...] = normed
    queries = mm6(normed[:16], w_query[...])
    keyval = mm6(normed, w_keyval[...])
    d_bottleneck = mm6_t(cotangent[...], w_out[...])
    parts = (queries, keyval[:16, :512], keyval[:16, 512:], d_bottleneck)
    for h in range(HEADS):
        block = slice(128 * (h // 4), 128 * (h // 4) + 128)
        message[h] = sum(
            turn(part[:, block], 32 * (c - h % 4)) * lanes(c) for c, part in enumerate(parts)
        )
    for j in range(8):
        roots[2 * j : 2 * j + 2, :] = keyval[16:18, 128 * j : 128 * j + 128]
    for j in range(4):
        roots[16 + 2 * j : 18 + 2 * j, :] = normed[16:18, 128 * j : 128 * j + 128]


def message_kernel(main, roots, message, root_rows):
    block = lambda j: roots[:, 2 * j : 2 * j + 2, :].reshape(8, 128)
    for h in range(HEADS):
        side = turn(block(h // 4), -32 * (h % 4)) * lanes(0)
        side = side + turn(block(4 + h // 4), 32 - 32 * (h % 4)) * lanes(1)
        for half in range(2):
            message[2 * h + half, :16, :] = main[h]
            message[2 * h + half, 16:, :] = side
    for j in range(4):
        root_rows[:, 128 * j : 128 * j + 128] = block(8 + j)


def attend_kernel(half, got, message):
    at = pl.multiple_of(half[0] * 8, 8)
    mine = got[:, pl.ds(at, 8), :].reshape(256, 128)
    every = got[:, :16, :].reshape(512, 128)
    away = got[:, 16:, :].reshape(256, 128)
    queries = mine * lanes(0) * SCALE
    d_out = mine * lanes(3)

    def scores_of(keys, values):
        probs = softmax(mm6_t(queries, keys))
        d_probs = mm6_t(d_out, values)
        d_scores = probs * (d_probs - jnp.sum(probs * d_probs, axis=-1, keepdims=True))
        return probs, d_scores * SCALE

    probs, d_scores = scores_of(turn(every, -32), turn(every, 32))
    front = mm6(probs, turn(every, -64) * lanes(0)) + mm6(d_scores, every * lanes(1))
    back = t_mm6(d_scores, turn(mine, 64) * lanes(2)) + t_mm6(probs, d_out)
    probs, d_scores = scores_of(away, turn(away, 64))
    front = front + mm6(probs, turn(away, -32) * lanes(0))
    front = front + mm6(d_scores, turn(away, 32) * lanes(1))
    side = t_mm6(d_scores, mine * lanes(0)) + t_mm6(probs, turn(mine, 64) * lanes(1))
    message[:, :16, :] = back.reshape(N_LEAF, 16, 128)
    message[:, pl.ds(at, 8), :] = message[:, pl.ds(at, 8), :] + front.reshape(N_LEAF, 8, 128)
    message[:, 16:, :] = side.reshape(N_LEAF, 8, 128)


def unpack_kernel(got, bottleneck, d_queries, d_keyval, d_roots):
    for block in range(4):
        heads = [got[2 * h] + got[2 * h + 1] for h in range(4 * block, 4 * block + 4)]
        pick = lambda c, rows: sum(
            turn(heads[k][rows], 32 * (k - c)) * lanes(k) for k in range(4)
        )
        own, far = slice(0, 16), slice(16, 24)
        at = slice(128 * block, 128 * block + 128)
        bottleneck[:, at] = pick(0, own)
        d_queries[:, at] = pick(1, own)
        d_keyval[:, at] = pick(2, own)
        d_keyval[:, 512 + 128 * block : 640 + 128 * block] = pick(3, own)
        d_roots[:, 2 * block : 2 * block + 2, :] = pick(0, far).reshape(4, 2, 128)
        d_roots[:, 8 + 2 * block : 10 + 2 * block, :] = pick(1, far).reshape(4, 2, 128)


def upper_kernel(coarse, bottleneck, d_queries, rows, cotangent, w_out, output, grad_out, grad_query):
    output[...] = coarse[...] + mm(bottleneck[...], w_out[...])
    grad_out[...] = t_mm(bottleneck[...], cotangent[...])
    grad_query[...] = t_mm(rows[:16, :], d_queries[...])


def rms_backward(d_normed, values, gain):
    scale = inverse_rms(values)
    unit = values * scale
    d_unit = d_normed * gain
    d_values = scale * (d_unit - unit * jnp.mean(d_unit * unit, axis=-1, keepdims=True))
    return d_values, jnp.sum(d_normed * unit, axis=0, keepdims=True)


def backward_kernel(
    d_roots, d_queries, d_keyval, rows, coarse, cotangent, gain_coarse, w_query, w_keyval,
    w_three, w_two, w_one, w_out_leaf, w_qkv, gain_leaf,
    unit, packed, weights, attended, mixed, pre_one, pre_two, two,
    grad_keyval, grad_three, grad_two, grad_one, grad_out_leaf, grad_qkv, gains,
    d_coarse, d_two, d_packed, d_attended,
):
    far = jnp.sum(d_roots[...], axis=0)
    far = jnp.concatenate([far[2 * j : 2 * j + 2] for j in range(8)], axis=1)
    d_kv = jnp.concatenate([d_keyval[...], far, jnp.zeros((6, 1024), F32)], axis=0)
    grad_keyval[...] = t_mm(rows[...], d_kv)
    d_rows = mm_t(d_kv, w_keyval[...])
    top = coarse[...]
    d_top, gain_a = rms_backward(
        d_rows[:16] + mm_t(d_queries[...], w_query[...]), top, gain_coarse[...]
    )
    means = jnp.concatenate(
        [jnp.mean(top[8 * r : 8 * r + 8], axis=0, keepdims=True) for r in range(2)], axis=0
    )
    d_means, gain_b = rms_backward(d_rows[16:18], means, gain_coarse[...])
    d_means = d_means * 0.125
    d_means = jnp.concatenate(
        [jnp.broadcast_to(d_means[r : r + 1], (8, 512)) for r in range(2)], axis=0
    )
    put_blocks(d_coarse, cotangent[...] + d_top + d_means)
    gain_c = gain_a + gain_b

    d_top = jnp.concatenate([stride_get(d_coarse, a, 2) for a in range(2)], axis=0)
    for d in range(4):
        at = slice(384 * d, 384 * d + 384)
        grad_three[at, :] = t_mm(slot_three(two, d), d_top)
        part = mm_t(d_top, w_three[at, :])
        for a in range(2):
            stride_put(d_two, 2 * d + a, 8, part[8 * a : 8 * a + 8])
    pre = pre_two[...]
    gate = sigmoid(pre)
    d_pre = get_blocks(d_two) * (gate * (1.0 + pre * (1.0 - gate)))
    pre = pre_one[...]
    gate = sigmoid(pre)
    one = pre * gate
    parts = []
    for d in range(4):
        at = slice(256 * d, 256 * d + 256)
        grad_two[at, :] = t_mm(slot_two(one, d), d_pre)
        parts.append(mm_t(d_pre, w_two[at, :]).reshape(8, 1, 8, 256))
    d_one = jnp.concatenate(parts, axis=1).reshape(256, 256)
    d_pre = d_one * (gate * (1.0 + pre * (1.0 - gate)))
    joined = mixed[...]
    parts = []
    for d in range(4):
        at = slice(128 * d, 128 * d + 128)
        grad_one[at, :] = t_mm(slot_one(joined, d), d_pre)
        parts.append(mm_t(d_pre, w_one[at, :]).reshape(8, 1, 32, 128))
    d_mixed = jnp.concatenate(parts, axis=1).reshape(1024, 128)
    grad_out_leaf[...] = t_mm(attended[...], d_mixed)
    d_attended[...] = mm_t(d_mixed, w_out_leaf[...])

    def ball(step, carry):
        at = pl.ds(step * 128, 128)
        probs = weights[pl.ds(step * 512, 512), :]
        d_out = four(d_attended[at, :])
        d_probs = mm6_t(d_out, packed[at, 256:])
        d_scores = probs * (d_probs - jnp.sum(probs * d_probs, axis=-1, keepdims=True)) * SCALE
        wide = jnp.concatenate([d_scores[128 * h : 128 * h + 128] for h in range(4)], axis=1)
        d_packed[at, :128] = mm(wide, four(packed[at, 128:256]))
        d_packed[at, 128:256] = t_mm(d_scores, four(packed[at, :128]))
        d_packed[at, 256:] = t_mm(probs, d_out)
        return carry

    lax.fori_loop(0, 8, ball, 0)
    grad_qkv[...] = t_mm(unit[...] * gain_leaf[...], d_packed[...])
    d_normed = mm_t(d_packed[...], w_qkv[...])
    gains[...] = jnp.concatenate(
        [jnp.sum(d_normed * unit[...], axis=0, keepdims=True)]
        + [gain_c[:, 128 * j : 128 * j + 128] for j in range(4)]
        + [jnp.zeros((3, 128), F32)],
        axis=0,
    )


def call(kernel, outs, scratch=(), smem_first=False):
    shapes = [jax.ShapeDtypeStruct(shape, F32) for shape in outs]

    def run(*args):
        specs = [pl.BlockSpec(memory_space=pltpu.VMEM)] * len(args)
        if smem_first:
            specs[0] = pl.BlockSpec(memory_space=pltpu.SMEM)
        return pl.pallas_call(
            kernel,
            out_shape=shapes,
            in_specs=specs,
            out_specs=[pl.BlockSpec(memory_space=pltpu.VMEM)] * len(shapes),
            scratch_shapes=[pltpu.VMEM(shape, F32) for shape in scratch],
            compiler_params=pltpu.CompilerParams(vmem_limit_bytes=56 * 2**20),
        )(*args)

    return run


def shards(
    features, tree_order, gain_leaf, w_qkv, w_out_leaf, w_one, w_two, w_three, gain_coarse,
    w_query, w_keyval, w_out, cotangent,
):
    half = (lax.axis_index("x") % 2).astype(jnp.int32).reshape(1)
    gain_leaf = gain_leaf.reshape(1, 128)
    gain_coarse = gain_coarse.reshape(1, 512)
    saved_shapes = [
        (1024, 128), (1024, 384), (4096, 128), (1024, 128), (1024, 128), (256, 256), (64, 384),
        (3, 64, 128),
    ]
    *saved, coarse, rows, main, roots = call(
        forward_kernel,
        saved_shapes + [(16, 512), (24, 512), (HEADS, 16, 128), (24, 128)],
        [(1024, 128), (4, 16, 128)],
        True,
    )(
        tree_order, features, gain_leaf, w_qkv, w_out_leaf, w_one, w_two, w_three, gain_coarse,
        w_query, w_keyval, w_out, cotangent,
    )
    roots = lax.all_gather(roots, GRP, axis=0)
    message, root_rows = call(message_kernel, [(N_LEAF, 24, 128), (8, 512)])(main, roots)
    got = lax.all_to_all(message, LEAF, 0, 0, tiled=True)
    message = call(attend_kernel, [(N_LEAF, 24, 128)], (), True)(half, got)[0]
    got = lax.all_to_all(message, LEAF, 0, 0, tiled=True)
    bottleneck, d_queries, d_keyval, d_roots = call(
        unpack_kernel, [(16, 512), (16, 512), (16, 1024), (4, 16, 128)]
    )(got)
    d_roots = lax.all_to_all(d_roots, GRP, 0, 0, tiled=True)
    output, grad_out, grad_query = call(upper_kernel, [(16, 512), (512, 512), (512, 512)])(
        coarse, bottleneck, d_queries, rows, cotangent, w_out
    )
    grads = call(
        backward_kernel,
        [(512, 1024), (1536, 512), (1024, 384), (512, 256), (128, 128), (128, 384), (8, 128)],
        [(4, 16, 128), (3, 64, 128), (1024, 384), (1024, 128)],
    )(
        d_roots, d_queries, d_keyval, rows, coarse, cotangent, gain_coarse, w_query, w_keyval,
        w_three, w_two, w_one, w_out_leaf, w_qkv, gain_leaf, *saved,
    )
    grad_keyval, grad_three, grad_two, grad_one, grad_out_leaf, grad_qkv, gains = grads
    low = jnp.concatenate([grad_out_leaf, gains], axis=0)
    totals = lax.psum(
        (grad_qkv, low, grad_one, grad_two, grad_three, grad_query, grad_keyval, grad_out), ALL
    )
    low = totals[1]
    return (
        output,
        low[128],
        totals[0],
        low[:128],
        totals[2],
        totals[3],
        totals[4],
        low[129:133].reshape(512),
        totals[5],
        totals[6],
        totals[7],
    )


def solution(mesh):
    fine = Mesh(mesh.devices.reshape(2, 2, 2, 4, 4), ALL)
    cut = P(ALL, None)
    return jax.shard_map(
        shards,
        mesh=fine,
        in_specs=(cut, cut) + (P(),) * 10 + (cut,),
        out_specs=(cut,) + (P(),) * 10,
        check_vma=False,
    )
```

time: 389 us -> 309 us (0.79); the launches traced: 383 us -> 309 us
  matrix products: 84 us -> 0 us
  Pallas kernels: 4.86 us -> 64.3 us
  local copies, waits for them, and re-layouts: 50.1 us -> 17 us
  other arithmetic: 21.1 us -> 1.48 us
  blocking collectives: 8.43 us -> 23.2 us
  starting transfers between devices: 20.7 us -> 15 us
  waiting for transfers between devices: 178 us -> 173 us
    dot_general x40 -> x0, matrix products: 84 us -> none  [the longest x20 42.9 us: mm(): jnp.dot(left, right, precision=PREC, preferred_element_type=jnp.float32)]
    pallas_call x0 -> x6, Pallas kernels: none -> 64.3 us  [run(): pl.pallas_call(kernel, out_shape=shapes, in_specs=specs, out_specs=[pl.Bl...]
    reshape x21 -> x1, local copies, waits for them, and re-layouts: 14.1 us -> 1.25 us  [shards(): low[129:133].reshape(512)]
    all_to_all x0 -> x1, blocking collectives: none -> 12.8 us  [shards(): got = lax.all_to_all(message, LEAF, 0, 0, tiled=True)]
    all_to_all x2 -> x1, waiting for transfers between devices: 16 us -> 8.77 us  [shards(): got = lax.all_to_all(message, LEAF, 0, 0, tiled=True)]
    reduce_sum x8 -> x0, other arithmetic: 5.23 us -> none  [the longest x2 2.57 us: rms_scale(): values * lax.rsqrt(jnp.mean(values * values, axis=-1, keepdims=True) + 1e...]
    all_to_all x2 -> x1, starting transfers between devices: 12.9 us -> 7.67 us  [shards(): got = lax.all_to_all(message, LEAF, 0, 0, tiled=True)]
    gather x1 -> x0, local copies, waits for them, and re-layouts: 5.15 us -> none  [shards(): ordered = features[tree_order[0]]]
  transfers between devices with their start and end apart: 4 -> 3, of which waited for: 4 -> 3; matrix products, arithmetic and copies ran while one was open for 2% -> 0% of each run, Pallas kernels for 0% -> 1%
where the time goes in v2:
time: 309 us
  waiting for transfers between devices  173 us (56%)
  Pallas kernels  64.3 us (21%)
  blocking collectives  23.2 us (8%)
  local copies, waits for them, and re-layouts  17 us (6%)
  starting transfers between devices  15 us (5%)
  between operations  14.1 us (5%)
    psum x1, waiting for transfers between devices, shards(): lax.psum((grad_qkv, low, grad_one, grad_two, grad_three, grad_query, grad...  163 us
    pallas_call x6, Pallas kernels, run(): pl.pallas_call(kernel, out_shape=shapes, in_specs=specs, out_specs=[pl.Bl...  64.3 us
    unnamed x21, local copies, waits for them, and re-layouts  13 us
    all_to_all x1, blocking collectives, shards(): got = lax.all_to_all(message, LEAF, 0, 0, tiled=True)  12.8 us
    all_gather x1, blocking collectives, shards(): roots = lax.all_gather(roots, GRP, axis=0)  10.4 us
    all_to_all x1, waiting for transfers between devices, shards(): got = lax.all_to_all(message, LEAF, 0, 0, tiled=True)  8.77 us
    all_to_all x1, starting transfers between devices, shards(): got = lax.all_to_all(message, LEAF, 0, 0, tiled=True)  7.67 us
    all_to_all x1, starting transfers between devices, shards(): d_roots = lax.all_to_all(d_roots, GRP, 0, 0, tiled=True)  7.32 us
  transfers between devices with their start and end apart: 3, of which 3 were waited for; matrix products, arithmetic and copies ran while one was open for 0% of the time, Pallas kernels for 1%

profile of v2, /device:TPU:1, one launch (start us, length us, event | category | flops | bytes accessed | tf_op | source)
XLA Modules:
  0.0 308.5 jit_solution(5374611559807138795)
XLA Ops:
  7.2 26.4 %shard_map.212 = (f32[1024,128]{1,0:T(8,128)}, f32[1024,384]{1,0:T(8,128)}, f32[4096,128]{1,0:T(8,128)}, f32[1024,128]{1,0:T(8,128)}, f32[1024,128]{1,0:T(8,128)...) custom-call(s32[1,1024]{1,0:T(1,128)} %order.1, ...), custom_call_target="tpu_custom_call" | custom-call | tf_op jit(solution)/shard_map/pallas_call | solution.py:339
  33.6 10.4 %all-gather = f32[96,128]{1,0:T(8,128)} all-gather(f32[24,128]{1,0:T(8,128)} %get-tuple-element.40), channel_id=2, replica_groups=mesh['zh'=2,'co'=2,'zl'=2,'y'=4,'x'=4] {'zh','co'}, dimensions={0}, use_global_device_ids=true | all-gather | bytes 61440 | tf_op jit(solution)/shard_map/all_gather | solution.py:371
  44.0 1.8 shard_map.213
  45.7 7.7 %all-to-all-start = ((f32[32,24,128]{2,1,0:T(8,128)}), f32[32,24,128]{2,1,0:T(8,128)S(1)}, u32[]{:S(2)}, u32[]{:S(2)}) async-start(f32[32,24,128]{2,1,0:T(8,128)} %get-tuple-element.41), calls=%async_computation | async-start | bytes 786432 | tf_op jit(solution)/shard_map/all_to_all | solution.py:373
  53.4 8.8 %all-to-all-done.got = f32[32,24,128]{2,1,0:T(8,128)S(1)} async-done(((f32[32,24,128]{2,1,0:T(8,128)}), f32[32,24,128]{2,1,0:T(8,128)S(1)}, u32[]{:S(2)}, u32[]{:S(2)}) %all-to-all-start) | async-done | bytes 393248 | tf_op jit(solution)/shard_map/all_to_all | solution.py:373
  62.2 0.0 copy-start.3
  62.2 0.7 copy-done.3
  62.9 6.0 %shard_map.214 = f32[32,24,128]{2,1,0:T(8,128)} custom-call(s32[1]{0:T(128)} %bitcast.2.half, f32[32,24,128]{2,1,0:T(8,128)} %copy-done.3), custom_call_target="tpu_custom_call" | custom-call | tf_op jit(solution)/shard_map/pallas_call | solution.py:339
  69.0 12.8 %all_to_all.15.got = f32[32,24,128]{2,1,0:T(8,128)} all-to-all(f32[32,24,128]{2,1,0:T(8,128)} %shard_map.214), channel_id=1, replica_groups=mesh['zh'=2,'co'=2,'zl'=2,'y'=4,'x'=4] {'zl','y','x'}, dimensions={0} | all-to-all | bytes 786432 | tf_op jit(solution)/shard_map/all_to_all | solution.py:375
  81.8 1.8 shard_map.215
  83.6 7.3 %all-to-all-start.2 = ((f32[4,16,128]{2,1,0:T(8,128)}), f32[4,16,128]{2,1,0:T(8,128)S(1)}, u32[]{:S(2)}, u32[]{:S(2)}) async-start(f32[4,16,128]{2,1,0:T(8,128)} %get-tuple-element.46), calls=%async_computation.2 | async-start | bytes 65536 | tf_op jit(solution)/shard_map/all_to_all | solution.py:379
  91.0 0.0 all-reduce.3.cloned.1.call-start
  91.0 3.5 %shard_map.216 = (f32[16,512]{1,0:T(8,128)}, f32[512,512]{1,0:T(8,128)}, f32[512,512]{1,0:T(8,128)}) custom-call(f32[16,512]{1,0:T(8,128)} %get-tuple-element.38.coarse, f32[16,512]{1,0:T(8,128)} %get-tuple-element.42.bottleneck, f32[16,512]{1,0:T(8,128)} %get-tuple-element.43.d_queries, f32[24,512]{1,0:T(8,128)} %get-tuple-element.44.rows, ...), custom_call_target="tpu_custom_call" | custom-call | tf_op jit(solution)/shard_map/pallas_call | solution.py:339
  94.4 1.2 all-to-all-done.2.d_roots
  95.6 0.0 copy-start.6
  95.6 0.6 copy-done.6
  96.2 24.8 %shard_map.217 = (f32[512,1024]{1,0:T(8,128)}, f32[1536,512]{1,0:T(8,128)}, f32[1024,384]{1,0:T(8,128)}, f32[512,256]{1,0:T(8,128)}, f32[128,128]{1,0:T(8,128)}, /*index=5*/f32[128,384]{1,0:T(8,128)}, f32[8,128]{1,0:T(8,128)}) custom-call(f32[4,16,128]{2,1,0:T(8,128)} %copy-done.6, f32[16,512]{1,0:T(8,128)} %get-tuple-element.43.d_queries, ...), custom_call_target="tpu_custom_call" | custom-call | tf_op jit(solution)/shard_map/pallas_call | solution.py:339
  121.0 1.5 pad_maximum_fusion
  122.5 0.0 all-reduce.3.cloned.1.call-update
  122.5 163.5 %all-reduce.3.cloned.1.call-done = (f32[136,128]{1,0:T(8,128)}, f32[128,384]{1,0:T(8,128)}, f32[512,256]{1,0:T(8,128)}, f32[1024,384]{1,0:T(8,128)}, f32[1536,51...) async-done(((f32[136,128]{1,0:T(8,128)}, f32[128,384]{1,0:T(8,128)}, f32[512,256]{1,0:T(8,128)}, f32[1024,384]{1,0:T(8,128)}, ...) | async-done | bytes 9703440 | tf_op jit(solution)/shard_map/psum | solution.py:393
  286.0 0.0 copy-start.2
  286.0 1.3 slice_bitcast_fusion.1
  287.3 1.2 slice_bitcast_fusion
  288.6 1.5 slice.13
  290.1 1.6 copy.32
  291.7 0.0 copy-start
  291.7 2.0 copy.33
  293.7 0.0 copy-done.2
  293.7 1.1 copy.34
  294.8 0.0 copy-done
  294.8 0.0 copy-start.5
  294.8 1.7 copy.35
  296.5 0.3 copy-done.5
  296.8 0.0 copy-start.1
  296.8 1.0 copy.36
  297.8 1.0 copy-done.1
  298.8 0.0 copy-start.4
  298.8 1.3 copy.37
  300.1 0.6 copy-done.4
  300.7 1.0 copy.38
Async XLA Ops:
  45.7 16.5 %all-to-all-start = ((f32[32,24,128]{2,1,0:T(8,128)}), f32[32,24,128]{2,1,0:T(8,128)S(1)}, u32[]{:S(2)}, u32[]{:S(2)}) async-start(f32[32,24,128]{2,1,0:T(8,128)} %get-tuple-element.41), calls=%async_computation | async-start | bytes 786432 | tf_op jit(solution)/shard_map/all_to_all | solution.py:373
  62.2 0.7 copy-start.3
  83.6 12.0 %all-to-all-start.2 = ((f32[4,16,128]{2,1,0:T(8,128)}), f32[4,16,128]{2,1,0:T(8,128)S(1)}, u32[]{:S(2)}, u32[]{:S(2)}) async-start(f32[4,16,128]{2,1,0:T(8,128)} %get-tuple-element.46), calls=%async_computation.2 | async-start | bytes 65536 | tf_op jit(solution)/shard_map/all_to_all | solution.py:379
  91.0 195.1 %all-reduce.3.cloned.1.call-start = ((), (), s32[]{:S(2)}) async-start(), calls=%async_computation.3 | async-start | bytes 19406848 | tf_op jit(solution)/shard_map/psum | solution.py:393
  95.6 0.6 copy-start.6
  286.0 7.7 %copy-start.2 = (f32[1024,384]{1,0:T(8,128)S(1)}, f32[1024,384]{1,0:T(8,128)}, u32[]{:S(2)}) copy-start(f32[1024,384]{1,0:T(8,128)} %get-tuple-element.78) | copy-start | bytes 4718596
  291.7 3.2 %copy-start = (f32[1536,512]{1,0:T(8,128)S(1)}, f32[1536,512]{1,0:T(8,128)}, u32[]{:S(2)}) copy-start(f32[1536,512]{1,0:T(8,128)} %get-tuple-element.79) | copy-start | bytes 9437188
  294.8 2.0 copy-start.5
  296.8 2.0 copy-start.1
  298.8 2.0 copy-start.4
Sparse Core Ops, SparseCore 0:
  122.7 163.3 all-reduce.2

commit v3 on v2

--- a/solution.py
+++ b/solution.py
@@ -9,6 +9,7 @@
 GRP = ("zh", "co")
 LEAF = ("zl", "y", "x")
 ALL = GRP + LEAF
+CHIPS = ("zh",) + LEAF
 N_LEAF = 32
 HEADS = 16
 SCALE = 32 ** (-0.5)
@@ -181,7 +182,10 @@
         roots[16 + 2 * j : 18 + 2 * j, :] = normed[16:18, 128 * j : 128 * j + 128]
 
 
-def message_kernel(main, roots, message, root_rows):
+def message_kernel(group, main, roots, one, two, three, message, root_rows, sorted_roots):
+    for k, part in enumerate((roots, one, two, three)):
+        sorted_roots[group[0] ^ k] = part[...]
+    roots = sorted_roots
     block = lambda j: roots[:, 2 * j : 2 * j + 2, :].reshape(8, 128)
     for h in range(HEADS):
         side = turn(block(h // 4), -32 * (h % 4)) * lanes(0)
@@ -219,26 +223,55 @@
     message[:, 16:, :] = side.reshape(N_LEAF, 8, 128)
 
 
-def unpack_kernel(got, bottleneck, d_queries, d_keyval, d_roots):
+def unpack_kernel(got, rows, root_rows, cotangent, bottleneck, d_queries, d_keyval, d_roots, pack):
+    pack[16:, :1024] = jnp.zeros((8, 1024), F32)
+    pack[16:, 2560:] = jnp.zeros((8, 512), F32)
+    pack[:16, 2048:2560] = rows[:16, :]
+    pack[16:, 2048:2560] = root_rows[...]
+    pack[:16, 2560:] = cotangent[...]
     for block in range(4):
         heads = [got[2 * h] + got[2 * h + 1] for h in range(4 * block, 4 * block + 4)]
         pick = lambda c, rows: sum(
             turn(heads[k][rows], 32 * (k - c)) * lanes(k) for k in range(4)
         )
         own, far = slice(0, 16), slice(16, 24)
-        at = slice(128 * block, 128 * block + 128)
-        bottleneck[:, at] = pick(0, own)
-        d_queries[:, at] = pick(1, own)
-        d_keyval[:, at] = pick(2, own)
-        d_keyval[:, 512 + 128 * block : 640 + 128 * block] = pick(3, own)
-        d_roots[:, 2 * block : 2 * block + 2, :] = pick(0, far).reshape(4, 2, 128)
-        d_roots[:, 8 + 2 * block : 10 + 2 * block, :] = pick(1, far).reshape(4, 2, 128)
-
-
-def upper_kernel(coarse, bottleneck, d_queries, rows, cotangent, w_out, output, grad_out, grad_query):
+        for c, ref in enumerate((bottleneck, d_queries, d_keyval, d_keyval)):
+            at = 128 * block + (512 if c == 3 else 0)
+            value = pick(c, own)
+            ref[:, at : at + 128] = value
+            pack[:16, 512 * c + 128 * block : 512 * c + 128 * block + 128] = value
+        for c in range(2):
+            value = pick(c, far)
+            at = 8 * c + 2 * block
+            d_roots[:, at : at + 2, :] = value.reshape(4, 2, 128)
+            at = 1024 + 512 * c + 128 * block
+            pack[16:, at : at + 128] = value
+
+
+def upper_kernel(core, coarse, bottleneck, w_out, mine, other, output, grads):
     output[...] = coarse[...] + mm(bottleneck[...], w_out[...])
-    grad_out[...] = t_mm(bottleneck[...], cotangent[...])
-    grad_query[...] = t_mm(rows[:16, :], d_queries[...])
+    both = lambda at, width: jnp.concatenate(
+        [mine[:, pl.ds(at, width)], other[:, pl.ds(at, width)]], axis=0
+    )
+    half = lambda at, width: both(pl.multiple_of(at + core[0] * width, 128), width)
+    normed = both(2048, 512)
+    grads[:, :256] = t_mm(both(0, 512), half(2560, 256))
+    grads[:, 256:512] = t_mm(normed, half(512, 256))
+    grads[:, 512:] = t_mm(normed, half(1024, 512))
+
+
+def assemble_upper_kernel(core, mine, other, grad_query, grad_keyval, grad_out):
+    def fill(half, source):
+        grad_out[:, 256 * half : 256 * half + 256] = source[:, :256]
+        grad_query[:, 256 * half : 256 * half + 256] = source[:, 256:512]
+        grad_keyval[:, 512 * half : 512 * half + 512] = source[:, 512:]
+
+    for half in range(2):
+
+        @pl.when(core[0] == half)
+        def _():
+            fill(half, mine)
+            fill(1 - half, other)
 
 
 def rms_backward(d_normed, values, gain):
@@ -250,16 +283,27 @@
 
 
 def backward_kernel(
-    d_roots, d_queries, d_keyval, rows, coarse, cotangent, gain_coarse, w_query, w_keyval,
+    group, d_roots, roots_one, roots_two, roots_three, d_queries, d_keyval, rows, coarse, cotangent, gain_coarse, w_query, w_keyval,
     w_three, w_two, w_one, w_out_leaf, w_qkv, gain_leaf,
     unit, packed, weights, attended, mixed, pre_one, pre_two, two,
-    grad_keyval, grad_three, grad_two, grad_one, grad_out_leaf, grad_qkv, gains,
+    keep, send,
     d_coarse, d_two, d_packed, d_attended,
 ):
-    far = jnp.sum(d_roots[...], axis=0)
+    def put(half, chips, at, value):
+        chips, at = pl.ds(*chips), pl.ds(*at)
+
+        @pl.when(core == half)
+        def _():
+            keep[chips, at, :] = value
+
+        @pl.when(core != half)
+        def _():
+            send[chips, at, :] = value
+
+    core = group[0] % 2
+    far = sum(ref[group[0]] for ref in (d_roots, roots_one, roots_two, roots_three))
     far = jnp.concatenate([far[2 * j : 2 * j + 2] for j in range(8)], axis=1)
     d_kv = jnp.concatenate([d_keyval[...], far, jnp.zeros((6, 1024), F32)], axis=0)
-    grad_keyval[...] = t_mm(rows[...], d_kv)
     d_rows = mm_t(d_kv, w_keyval[...])
     top = coarse[...]
     d_top, gain_a = rms_backward(
@@ -279,7 +323,10 @@
     d_top = jnp.concatenate([stride_get(d_coarse, a, 2) for a in range(2)], axis=0)
     for d in range(4):
         at = slice(384 * d, 384 * d + 384)
-        grad_three[at, :] = t_mm(slot_three(two, d), d_top)
+        grad = t_mm(slot_three(two, d), d_top)
+        for i in range(4):
+            block = grad[:, 128 * i : 128 * i + 128].reshape(16, 24, 128)
+            put(i // 2, (16 * d, 16), (24 * (i % 2), 24), block)
         part = mm_t(d_top, w_three[at, :])
         for a in range(2):
             stride_put(d_two, 2 * d + a, 8, part[8 * a : 8 * a + 8])
@@ -292,7 +339,10 @@
     parts = []
     for d in range(4):
         at = slice(256 * d, 256 * d + 256)
-        grad_two[at, :] = t_mm(slot_two(one, d), d_pre)
+        grad = t_mm(slot_two(one, d), d_pre)
+        for i in range(3):
+            block = grad[:, 128 * i : 128 * i + 128].reshape(32, 8, 128)
+            put(d // 2, (32 * (d % 2), 32), (48 + 8 * i, 8), block)
         parts.append(mm_t(d_pre, w_two[at, :]).reshape(8, 1, 8, 256))
     d_one = jnp.concatenate(parts, axis=1).reshape(256, 256)
     d_pre = d_one * (gate * (1.0 + pre * (1.0 - gate)))
@@ -300,10 +350,12 @@
     parts = []
     for d in range(4):
         at = slice(128 * d, 128 * d + 128)
-        grad_one[at, :] = t_mm(slot_one(joined, d), d_pre)
+        grad = t_mm(slot_one(joined, d), d_pre)
+        for i in range(2):
+            put(i, (16 * d, 16), (72, 8), grad[:, 128 * i : 128 * i + 128].reshape(16, 8, 128))
         parts.append(mm_t(d_pre, w_one[at, :]).reshape(8, 1, 32, 128))
     d_mixed = jnp.concatenate(parts, axis=1).reshape(1024, 128)
-    grad_out_leaf[...] = t_mm(attended[...], d_mixed)
+    grad_out_leaf = t_mm(attended[...], d_mixed)
     d_attended[...] = mm_t(d_mixed, w_out_leaf[...])
 
     def ball(step, carry):
@@ -319,17 +371,55 @@
         return carry
 
     lax.fori_loop(0, 8, ball, 0)
-    grad_qkv[...] = t_mm(unit[...] * gain_leaf[...], d_packed[...])
+    grad_qkv = t_mm(unit[...] * gain_leaf[...], d_packed[...])
+    blocks = [grad_qkv[:, 128 * i : 128 * i + 128] for i in range(3)] + [grad_out_leaf]
+    for i, block in enumerate(blocks):
+        put(i // 2, (16 * (i % 2), 16), (80, 8), block.reshape(16, 8, 128))
     d_normed = mm_t(d_packed[...], w_qkv[...])
-    gains[...] = jnp.concatenate(
+    gains = jnp.concatenate(
         [jnp.sum(d_normed * unit[...], axis=0, keepdims=True)]
         + [gain_c[:, 128 * j : 128 * j + 128] for j in range(4)]
         + [jnp.zeros((3, 128), F32)],
         axis=0,
     )
-
-
-def call(kernel, outs, scratch=(), smem_first=False):
+    put(0, (32, 1), (80, 8), gains.reshape(1, 8, 128))
+    put(0, (33, 31), (80, 8), jnp.zeros((31, 8, 128), F32))
+    put(1, (32, 32), (80, 8), jnp.zeros((32, 8, 128), F32))
+
+
+def assemble_kernel(
+    core, mine, other,
+    gain_leaf, gain_coarse, grad_qkv, grad_out_leaf, grad_one, grad_two, grad_three,
+):
+    def fill(half, source):
+        for i in range(2):
+            at = 256 * half + 128 * i
+            grad_three[:, at : at + 128] = source[:, 24 * i : 24 * i + 24, :].reshape(1536, 128)
+        for i in range(3):
+            block = source[:, 48 + 8 * i : 56 + 8 * i, :].reshape(512, 128)
+            grad_two[512 * half : 512 * half + 512, 128 * i : 128 * i + 128] = block
+        grad_one[:, 128 * half : 128 * half + 128] = source[:, 72:80, :].reshape(512, 128)
+        first = source[0:16, 80:88, :].reshape(128, 128)
+        second = source[16:32, 80:88, :].reshape(128, 128)
+        if half == 0:
+            grad_qkv[:, :128] = first
+            grad_qkv[:, 128:256] = second
+            gain_leaf[...] = source[32, 80, :]
+            for i in range(4):
+                gain_coarse[128 * i : 128 * i + 128] = source[32, 81 + i, :]
+        else:
+            grad_qkv[:, 256:] = first
+            grad_out_leaf[...] = second
+
+    for half in range(2):
+
+        @pl.when(core[0] == half)
+        def _():
+            fill(half, mine)
+            fill(1 - half, other)
+
+
+def call(kernel, outs, scratch=(), smem_first=False, cost=None):
     shapes = [jax.ShapeDtypeStruct(shape, F32) for shape in outs]
 
     def run(*args):
@@ -342,10 +432,20 @@
             in_specs=specs,
             out_specs=[pl.BlockSpec(memory_space=pltpu.VMEM)] * len(shapes),
             scratch_shapes=[pltpu.VMEM(shape, F32) for shape in scratch],
+            cost_estimate=cost,
             compiler_params=pltpu.CompilerParams(vmem_limit_bytes=56 * 2**20),
         )(*args)
 
     return run
+
+
+def group_swaps(value):
+    return [lax.ppermute(value, GRP, [(i, i ^ k) for i in range(4)]) for k in range(1, 4)]
+
+
+def spread(value, axes, parts):
+    wide = jnp.broadcast_to(value[None], (parts,) + value.shape)
+    return lax.all_to_all(wide, axes, 0, 0, tiled=True)
 
 
 def shards(
@@ -353,6 +453,8 @@
     w_query, w_keyval, w_out, cotangent,
 ):
     half = (lax.axis_index("x") % 2).astype(jnp.int32).reshape(1)
+    group = lax.axis_index(GRP).astype(jnp.int32).reshape(1)
+    core = lax.axis_index("co").astype(jnp.int32).reshape(1)
     gain_leaf = gain_leaf.reshape(1, 128)
     gain_coarse = gain_coarse.reshape(1, 512)
     saved_shapes = [
@@ -368,45 +470,48 @@
         tree_order, features, gain_leaf, w_qkv, w_out_leaf, w_one, w_two, w_three, gain_coarse,
         w_query, w_keyval, w_out, cotangent,
     )
-    roots = lax.all_gather(roots, GRP, axis=0)
-    message, root_rows = call(message_kernel, [(N_LEAF, 24, 128), (8, 512)])(main, roots)
+    message, root_rows = call(
+        message_kernel, [(N_LEAF, 24, 128), (8, 512)], [(4, 24, 128)], True
+    )(group, main, roots, *group_swaps(roots))
     got = lax.all_to_all(message, LEAF, 0, 0, tiled=True)
     message = call(attend_kernel, [(N_LEAF, 24, 128)], (), True)(half, got)[0]
     got = lax.all_to_all(message, LEAF, 0, 0, tiled=True)
-    bottleneck, d_queries, d_keyval, d_roots = call(
-        unpack_kernel, [(16, 512), (16, 512), (16, 1024), (4, 16, 128)]
-    )(got)
-    d_roots = lax.all_to_all(d_roots, GRP, 0, 0, tiled=True)
-    output, grad_out, grad_query = call(upper_kernel, [(16, 512), (512, 512), (512, 512)])(
-        coarse, bottleneck, d_queries, rows, cotangent, w_out
-    )
-    grads = call(
+    bottleneck, d_queries, d_keyval, d_roots, pack = call(
+        unpack_kernel, [(16, 512), (16, 512), (16, 1024), (4, 16, 128), (24, 3072)]
+    )(got, rows, root_rows, cotangent)
+    swap = lambda v: lax.ppermute(v, "co", [(0, 1), (1, 0)])
+    output, upper = call(upper_kernel, [(16, 512), (512, 1024)], (), True)(
+        core, coarse, bottleneck, w_out, pack, swap(pack)
+    )
+    upper, *far = lax.optimization_barrier((upper, *group_swaps(d_roots)))
+    upper = lax.all_to_all(upper.reshape(64, 8, 1024), CHIPS, 0, 0, tiled=True)
+    keep, send = call(
         backward_kernel,
-        [(512, 1024), (1536, 512), (1024, 384), (512, 256), (128, 128), (128, 384), (8, 128)],
+        [(64, 88, 128), (64, 88, 128)],
         [(4, 16, 128), (3, 64, 128), (1024, 384), (1024, 128)],
+        True,
+        pl.CostEstimate(flops=12_000_000_000, bytes_accessed=20_000_000, transcendentals=0),
     )(
-        d_roots, d_queries, d_keyval, rows, coarse, cotangent, gain_coarse, w_query, w_keyval,
-        w_three, w_two, w_one, w_out_leaf, w_qkv, gain_leaf, *saved,
-    )
-    grad_keyval, grad_three, grad_two, grad_one, grad_out_leaf, grad_qkv, gains = grads
-    low = jnp.concatenate([grad_out_leaf, gains], axis=0)
-    totals = lax.psum(
-        (grad_qkv, low, grad_one, grad_two, grad_three, grad_query, grad_keyval, grad_out), ALL
-    )
-    low = totals[1]
-    return (
-        output,
-        low[128],
-        totals[0],
-        low[:128],
-        totals[2],
-        totals[3],
-        totals[4],
-        low[129:133].reshape(512),
-        totals[5],
-        totals[6],
-        totals[7],
-    )
+        group, d_roots, *far, d_queries, d_keyval, rows, coarse, cotangent,
+        gain_coarse, w_query, w_keyval, w_three, w_two, w_one, w_out_leaf, w_qkv, gain_leaf,
+        *saved,
+    )
+    send, upper = lax.optimization_barrier((send, upper))
+    upper = spread(jnp.sum(upper, axis=0), CHIPS, 64).reshape(512, 1024)
+    late, upper = lax.optimization_barrier((keep + swap(send), upper))
+    late = jnp.sum(lax.all_to_all(late, CHIPS, 0, 0, tiled=True), axis=0)
+    late = spread(late, CHIPS, 64)
+    upper = call(assemble_upper_kernel, [(512, 512), (512, 1024), (512, 512)], (), True)(
+        core, upper, swap(upper)
+    )
+    late, *upper = lax.optimization_barrier((late, *upper))
+    gain_leaf, gain_coarse, *rest = call(
+        assemble_kernel,
+        [(128,), (512,), (128, 384), (128, 128), (512, 256), (1024, 384), (1536, 512)],
+        (),
+        True,
+    )(core, late, swap(late))
+    return (output, gain_leaf, *rest, gain_coarse, *upper)
 
 
 def solution(mesh):

time: 309 us -> 272 us (0.88)
  waiting for transfers between devices: 173 us -> 73 us
  blocking collectives: 23.2 us -> 55.9 us
  starting transfers between devices: 15 us -> 47.1 us
  Pallas kernels: 64.3 us -> 80 us
  between operations: 14.1 us -> 0.76 us
  local copies, waits for them, and re-layouts: 17 us -> 8.95 us
  other arithmetic: 1.48 us -> 5.1 us
    psum x1 -> x0, waiting for transfers between devices: 163 us -> none  [shards(): lax.psum((grad_qkv, low, grad_one, grad_two, grad_three, grad_query, grad...]
    all_to_all x1 -> x3, waiting for transfers between devices: 1.2 us -> 52.2 us  [the longest x2 52 us: spread(): return lax.all_to_all(wide, axes, 0, 0, tiled=True)]
    all_to_all x0 -> x1, blocking collectives: none -> 42.9 us  [shards(): late = jnp.sum(lax.all_to_all(late, CHIPS, 0, 0, tiled=True), axis=0)]
    ppermute x0 -> x10, starting transfers between devices: none -> 18.6 us  [the longest x4 9.41 us: shards(): swap = lambda v: lax.ppermute(v, 'co', [(0, 1), (1, 0)])]
    pallas_call x6 -> x8, Pallas kernels: 64.3 us -> 80 us  [run(): pl.pallas_call(kernel, out_shape=shapes, in_specs=specs, out_specs=[pl.Bl...]
    all_to_all x1 -> x3, starting transfers between devices: 7.32 us -> 20.9 us  [the longest x2 15.5 us: spread(): return lax.all_to_all(wide, axes, 0, 0, tiled=True)]
    ppermute x0 -> x10, waiting for transfers between devices: none -> 12.7 us  [the longest x4 8.91 us: shards(): swap = lambda v: lax.ppermute(v, 'co', [(0, 1), (1, 0)])]
    all_gather x1 -> x0, blocking collectives: 10.4 us -> none  [shards(): roots = lax.all_gather(roots, GRP, axis=0)]
  transfers between devices with their start and end apart: 3 -> 14, of which waited for: 3 -> 8; matrix products, arithmetic and copies ran while one was open for 0% -> 2% of each run, Pallas kernels for 1% -> 14%
where the time goes in v3:
time: 272 us; the launch traced here: 271 us
  Pallas kernels  80 us (29%)
  waiting for transfers between devices  73 us (27%)
  blocking collectives  55.9 us (21%)
  starting transfers between devices  47.1 us (17%)
  local copies, waits for them, and re-layouts  8.95 us (3%)
  other arithmetic  5.1 us (2%)
    pallas_call x8, Pallas kernels, run(): pl.pallas_call(kernel, out_shape=shapes, in_specs=specs, out_specs=[pl.Bl...  80 us
    all_to_all x2, waiting for transfers between devices, spread(): return lax.all_to_all(wide, axes, 0, 0, tiled=True)  52 us
    all_to_all x1, blocking collectives, shards(): late = jnp.sum(lax.all_to_all(late, CHIPS, 0, 0, tiled=True), axis=0)  42.9 us
    all_to_all x2, starting transfers between devices, spread(): return lax.all_to_all(wide, axes, 0, 0, tiled=True)  15.5 us
    all_to_all x1, blocking collectives, shards(): got = lax.all_to_all(message, LEAF, 0, 0, tiled=True)  13 us
    ppermute x4, starting transfers between devices, shards(): swap = lambda v: lax.ppermute(v, 'co', [(0, 1), (1, 0)])  9.41 us
    ppermute x6, starting transfers between devices, group_swaps(): lax.ppermute(value, GRP, [(i, i ^ k) for i in range(4)])  9.2 us
    ppermute x4, waiting for transfers between devices, shards(): swap = lambda v: lax.ppermute(v, 'co', [(0, 1), (1, 0)])  8.91 us
  transfers between devices with their start and end apart: 14, of which 8 were waited for; matrix products, arithmetic and copies ran while one was open for 2% of the time, Pallas kernels for 14%

profile of v3, /device:TPU:1, one launch (start us, length us, event | category | flops | bytes accessed | tf_op | source)
XLA Modules:
  0.0 270.9 jit_solution(15396856626126391565)
XLA Ops:
  0.6 26.4 %shard_map.212 = (f32[1024,128]{1,0:T(8,128)}, f32[1024,384]{1,0:T(8,128)}, f32[4096,128]{1,0:T(8,128)}, f32[1024,128]{1,0:T(8,128)}, f32[1024,128]{1,0:T(8,128)...) custom-call(s32[1,1024]{1,0:T(1,128)} %order.1, ...), custom_call_target="tpu_custom_call" | custom-call | tf_op jit(solution)/shard_map/pallas_call | solution.py:429
  27.1 5.1 %collective-permute-start.2 = (f32[24,128]{1,0:T(8,128)}, f32[24,128]{1,0:T(8,128)S(1)}, u32[]{:S(2)}, u32[]{:S(2)}) collective-permute-start(f32[24,128]{1,0:T(8,128)} %get-tuple-element.58.roots), channel_id=1, source_target_pairs={{0,96},{32,64},{64,32},{96,0},{1,97},{33,65},{65,33},{97,1},{2,98}... | collective-permute-start | bytes 36872 | tf_op jit(solution)/shard_map/ppermute | solution.py:443
  32.2 0.5 collective-permute-start
  32.6 1.1 collective-permute-done.2.three
  33.8 2.7 collective-permute-done.1.two
  36.4 0.0 collective-permute-done.one
  36.4 0.6 copy-done.6
  37.0 1.8 shard_map.213
  38.8 7.7 %all-to-all-start = ((f32[32,24,128]{2,1,0:T(8,128)}), f32[32,24,128]{2,1,0:T(8,128)S(1)}, u32[]{:S(2)}, u32[]{:S(2)}) async-start(f32[32,24,128]{2,1,0:T(8,128)} %get-tuple-element.59), calls=%async_computation | async-start | bytes 786432 | tf_op jit(solution)/shard_map/all_to_all | solution.py:476
  46.5 8.1 %all-to-all-done.got = f32[32,24,128]{2,1,0:T(8,128)S(1)} async-done(((f32[32,24,128]{2,1,0:T(8,128)}), f32[32,24,128]{2,1,0:T(8,128)S(1)}, u32[]{:S(2)}, u32[]{:S(2)}) %all-to-all-start) | async-done | bytes 393248 | tf_op jit(solution)/shard_map/all_to_all | solution.py:476
  54.6 0.7 copy-done.3
  55.4 6.0 %shard_map.214 = f32[32,24,128]{2,1,0:T(8,128)} custom-call(s32[1]{0:T(128)} %bitcast.3.half, f32[32,24,128]{2,1,0:T(8,128)} %copy-done.3), custom_call_target="tpu_custom_call" | custom-call | tf_op jit(solution)/shard_map/pallas_call | solution.py:429
  61.4 13.0 %all_to_all.30.got = f32[32,24,128]{2,1,0:T(8,128)} all-to-all(f32[32,24,128]{2,1,0:T(8,128)} %shard_map.214), channel_id=1, replica_groups=mesh['zh'=2,'co'=2,'zl'=2,'y'=4,'x'=4] {'zl','y','x'}, dimensions={0} | all-to-all | bytes 786432 | tf_op jit(solution)/shard_map/all_to_all | solution.py:478
  74.4 2.0 shard_map.215
  76.4 3.6 %collective-permute-start.3 = (f32[24,3072]{1,0:T(8,128)}, f32[24,3072]{1,0:T(8,128)S(1)}, u32[]{:S(2)}, u32[]{:S(2)}) collective-permute-start(f32[24,3072]{1,0:T(8,128)} %get-tuple-element.63.mine), channel_id=1, source_target_pairs={{0,32},{32,0},{1,33},{33,1},{2,34},{34,2},{3,35},{35,3},{4,36},{36... | collective-permute-start | bytes 884744 | tf_op jit(solution)/shard_map/ppermute | solution.py:482
  80.0 0.9 collective-permute-start.6
  80.9 1.9 collective-permute-start.5
  82.8 0.8 collective-permute-start.4
  83.6 0.7 copy-done.4
  84.3 4.0 %shard_map.216 = (f32[16,512]{1,0:T(8,128)}, f32[512,1024]{1,0:T(8,128)}) custom-call(s32[1]{0:T(128)} %bitcast.core, f32[16,512]{1,0:T(8,128)} %get-tuple-element.56.coarse, f32[16,512]{1,0:T(8,128)} %get-tuple-element.62.bottleneck, f32[512,512]{1,0:T(8,128)} %w_out.3, f32[24,3072]{1,0:T(8,128)} %get-tuple-element.63.mine, f32[24,3072]{1,0:T(8,128)} %copy-done.4), custom_call_target="tpu_custom_call" | custom-call | tf_op jit(solution)/shard_map/pallas_call | solution.py:429
  88.3 0.0 collective-permute-done.6.roots_three
  88.3 0.0 collective-permute-done.4.roots_one
  88.4 0.0 copy-start.10
  88.4 0.6 copy-done.8
  88.9 0.0 copy-done.9
  89.0 0.0 copy-done.10
  89.0 5.4 %all-to-all-start.2 = ((f32[64,8,1024]{2,1,0:T(8,128)}), f32[64,8,1024]{2,1,0:T(8,128)S(1)}, u32[]{:S(2)}, u32[]{:S(2)}) async-start(f32[64,8,1024]{2,1,0:T(8,128)} %bitcast.7), calls=%async_computation.2 | async-start | bytes 4194304 | tf_op jit(solution)/shard_map/all_to_all | solution.py:487
  94.4 29.5 %shard_map.217 = (f32[64,88,128]{2,1,0:T(8,128)}, f32[64,88,128]{2,1,0:T(8,128)}) custom-call(s32[1]{0:T(128)} %bitcast.4.group, f32[4,16,128]{2,1,0:T(8,128)} %get-tuple-element.65.d_roots, f32[4,16,128]{2,1,0:T(8,128)} %copy-done.10, f32[4,16,128]{2,1,0:T(8,128)} %copy-done.9, f32[4,16,128]{2,1,0:T(8,128)} %copy-done.8, ...), custom_call_target="tpu_custom_call" | custom-call | flops 12000000000 | bytes 20000000 | tf_op jit(solution)/shard_map/pallas_call | solution.py:429
  123.9 0.2 all-to-all-done.2
  124.1 1.4 collective-permute-start.7
  125.5 0.1 reduce_sum.18
  125.6 1.6 broadcast_in_dim.4
  127.2 9.1 %all-to-all-start.3 = ((f32[64,8,1024]{2,1,0:T(8,128)}), f32[64,8,1024]{2,1,0:T(8,128)}, u32[]{:S(2)}, u32[]{:S(2)}) async-start(f32[64,8,1024]{2,1,0:T(8,128)} %broadcast_in_dim.4), calls=%async_computation.3 | async-start | bytes 4194304 | tf_op jit(solution)/shard_map/all_to_all | solution.py:448
  136.3 3.0 %add.12 = f32[64,88,128]{2,1,0:T(8,128)S(1)} add(f32[64,88,128]{2,1,0:T(8,128)} %get-tuple-element.80, f32[64,88,128]{2,1,0:T(8,128)} %collective-permute-done.7) | non-fusion elementwise | flops 720896 | bytes 8650752 | tf_op jit(solution)/shard_map/add | solution.py:501
  139.2 26.5 %all-to-all-done.3 = f32[64,8,1024]{2,1,0:T(8,128)} async-done(((f32[64,8,1024]{2,1,0:T(8,128)}), f32[64,8,1024]{2,1,0:T(8,128)}, u32[]{:S(2)}, u32[]{:S(2)}) %all-to-all-start.3) | async-done | bytes 2097184 | tf_op jit(solution)/shard_map/all_to_all | solution.py:448
  165.8 42.9 %all_to_all.31 = f32[64,88,128]{2,1,0:T(8,128)} all-to-all(f32[64,88,128]{2,1,0:T(8,128)S(1)} %add.12), channel_id=1, replica_groups=mesh['zh'=2,'co'=2,'zl'=2,'y'=4,'x'=4] {'zh','zl','y','x'}, dimensions={0} | all-to-all | bytes 5767168 | tf_op jit(solution)/shard_map/all_to_all | solution.py:502
  208.7 2.0 reduce_sum.19
  210.7 1.8 broadcast_in_dim.5
  212.4 6.4 %all-to-all-start.5 = ((f32[64,88,128]{2,1,0:T(8,128)}), f32[64,88,128]{2,1,0:T(8,128)S(1)}, u32[]{:S(2)}, u32[]{:S(2)}) async-start(f32[64,88,128]{2,1,0:T(8,128)} %broadcast_in_dim.5), calls=%async_computation.5 | async-start | bytes 5767168 | tf_op jit(solution)/shard_map/all_to_all | solution.py:448
  218.8 1.2 collective-permute-start.8
  220.0 4.0 %collective-permute-done.8.other = f32[512,1024]{1,0:T(8,128)S(1)} collective-permute-done((f32[512,1024]{1,0:T(8,128)}, f32[512,1024]{1,0:T(8,128)S(1)}, u32[]{:S(2)}, u32[]{:S(2)}) %collective-permute-start.8) | collective-permute-done | bytes 2097184 | tf_op jit(solution)/shard_map/ppermute | solution.py:482
  224.0 1.4 copy-done.2
  225.4 4.5 %shard_map.218 = (f32[512,512]{1,0:T(8,128)}, f32[512,1024]{1,0:T(8,128)}, f32[512,512]{1,0:T(8,128)}) custom-call(s32[1]{0:T(128)} %bitcast.core, f32[512,1024]{1,0:T(8,128)} %bitcast.6.mine, f32[512,1024]{1,0:T(8,128)} %copy-done.2), custom_call_target="tpu_custom_call" | custom-call | tf_op jit(solution)/shard_map/pallas_call | solution.py:429
  229.9 25.5 %all-to-all-done.5.mine = f32[64,88,128]{2,1,0:T(8,128)S(1)} async-done(((f32[64,88,128]{2,1,0:T(8,128)}), f32[64,88,128]{2,1,0:T(8,128)S(1)}, u32[]{:S(2)}, u32[]{:S(2)}) %all-to-all-start.5) | async-done | bytes 2883616 | tf_op jit(solution)/shard_map/all_to_all | solution.py:448
  255.4 3.2 %collective-permute-start.9 = (f32[64,88,128]{2,1,0:T(8,128)S(1)}, f32[64,88,128]{2,1,0:T(8,128)S(1)}, u32[]{:S(2)}, u32[]{:S(2)}) collective-permute-start(f32[64,88,128]{2,1,0:T(8,128)S(1)} %all-to-all-done.5.mine), channel_id=1, source_target_pairs={{0,32},{32,0},{1,33},{33,1},{2,34},{34,2},{3,35},{35,3},{4,36},{36... | collective-permute-start | bytes 8650760 | tf_op jit(solution)/shard_map/ppermute | solution.py:482
  258.6 4.9 %collective-permute-done.9.other = f32[64,88,128]{2,1,0:T(8,128)S(1)} collective-permute-done((f32[64,88,128]{2,1,0:T(8,128)S(1)}, f32[64,88,128]{2,1,0:T(8,128)S(1)}, u32[]{:S(2)}, u32[]{:S(2)}) %collective-permute-start.9) | collective-permute-done | bytes 2883616 | tf_op jit(solution)/shard_map/ppermute | solution.py:482
  263.5 1.6 copy-done.1
  265.1 5.7 %shard_map.219 = (f32[128]{0:T(128)}, f32[512]{0:T(512)}, f32[128,384]{1,0:T(8,128)}, f32[128,128]{1,0:T(8,128)}, f32[512,256]{1,0:T(8,128)}, /*index=5*/f32[1024,384]{1,0:T(8,128)}, f32[1536,512]{1,0:T(8,128)}) custom-call(s32[1]{0:T(128)} %bitcast.core, f32[64,88,128]{2,1,0:T(8,128)} %copy-done, f32[64,88,128]{2,1,0:T(8,128)} %copy-done.1), custom_call_target="tpu_custom_call" | custom-call | tf_op jit(solution)/shard_map/pallas_call | solution.py:429
  (17 shorter events, 0.0 us)
Async XLA Ops:
  27.1 6.7 %collective-permute-start.2 = (f32[24,128]{1,0:T(8,128)}, f32[24,128]{1,0:T(8,128)S(1)}, u32[]{:S(2)}, u32[]{:S(2)}) collective-permute-start(f32[24,128]{1,0:T(8,128)} %get-tuple-element.58.roots), channel_id=1, source_target_pairs={{0,96},{32,64},{64,32},{96,0},{1,97},{33,65},{65,33},{97,1},{2,98}... | collective-permute-start | bytes 36872 | tf_op jit(solution)/shard_map/ppermute | solution.py:443
  32.2 4.3 %collective-permute-start.1 = (f32[24,128]{1,0:T(8,128)}, f32[24,128]{1,0:T(8,128)S(1)}, u32[]{:S(2)}, u32[]{:S(2)}) collective-permute-start(f32[24,128]{1,0:T(8,128)} %get-tuple-element.58.roots), channel_id=1, source_target_pairs={{0,64},{32,96},{64,0},{96,32},{1,65},{33,97},{65,1},{97,33},{2,66}... | collective-permute-start | bytes 36872 | tf_op jit(solution)/shard_map/ppermute | solution.py:443
  32.2 4.3 %collective-permute-start = (f32[24,128]{1,0:T(8,128)}, f32[24,128]{1,0:T(8,128)S(1)}, u32[]{:S(2)}, u32[]{:S(2)}) collective-permute-start(f32[24,128]{1,0:T(8,128)} %get-tuple-element.58.roots), channel_id=1, source_target_pairs={{0,32},{32,0},{64,96},{96,64},{1,33},{33,1},{65,97},{97,65},{2,34}... | collective-permute-start | bytes 36872 | tf_op jit(solution)/shard_map/ppermute | solution.py:443
  33.8 2.7 copy-start.5
  36.4 0.6 copy-start.6
  36.4 0.6 copy-start.7
  38.8 15.8 %all-to-all-start = ((f32[32,24,128]{2,1,0:T(8,128)}), f32[32,24,128]{2,1,0:T(8,128)S(1)}, u32[]{:S(2)}, u32[]{:S(2)}) async-start(f32[32,24,128]{2,1,0:T(8,128)} %get-tuple-element.59), calls=%async_computation | async-start | bytes 786432 | tf_op jit(solution)/shard_map/all_to_all | solution.py:476
  54.6 0.7 copy-start.3
  76.4 7.3 %collective-permute-start.3 = (f32[24,3072]{1,0:T(8,128)}, f32[24,3072]{1,0:T(8,128)S(1)}, u32[]{:S(2)}, u32[]{:S(2)}) collective-permute-start(f32[24,3072]{1,0:T(8,128)} %get-tuple-element.63.mine), channel_id=1, source_target_pairs={{0,32},{32,0},{1,33},{33,1},{2,34},{34,2},{3,35},{35,3},{4,36},{36... | collective-permute-start | bytes 884744 | tf_op jit(solution)/shard_map/ppermute | solution.py:482
  80.0 8.3 %collective-permute-start.6 = (f32[4,16,128]{2,1,0:T(8,128)}, f32[4,16,128]{2,1,0:T(8,128)S(1)}, u32[]{:S(2)}, u32[]{:S(2)}) collective-permute-start(f32[4,16,128]{2,1,0:T(8,128)} %get-tuple-element.65.d_roots), channel_id=1, source_target_pairs={{0,96},{32,64},{64,32},{96,0},{1,97},{33,65},{65,33},{97,1},{2,98}... | collective-permute-start | bytes 98312 | tf_op jit(solution)/shard_map/ppermute | solution.py:443
  80.9 7.4 %collective-permute-start.5 = (f32[4,16,128]{2,1,0:T(8,128)}, f32[4,16,128]{2,1,0:T(8,128)S(1)}, u32[]{:S(2)}, u32[]{:S(2)}) collective-permute-start(f32[4,16,128]{2,1,0:T(8,128)} %get-tuple-element.65.d_roots), channel_id=1, source_target_pairs={{0,64},{32,96},{64,0},{96,32},{1,65},{33,97},{65,1},{97,33},{2,66}... | collective-permute-start | bytes 98312 | tf_op jit(solution)/shard_map/ppermute | solution.py:443
  82.8 5.5 %collective-permute-start.4 = (f32[4,16,128]{2,1,0:T(8,128)}, f32[4,16,128]{2,1,0:T(8,128)S(1)}, u32[]{:S(2)}, u32[]{:S(2)}) collective-permute-start(f32[4,16,128]{2,1,0:T(8,128)} %get-tuple-element.65.d_roots), channel_id=1, source_target_pairs={{0,32},{32,0},{64,96},{96,64},{1,33},{33,1},{65,97},{97,65},{2,34}... | collective-permute-start | bytes 98312 | tf_op jit(solution)/shard_map/ppermute | solution.py:443
  83.6 0.7 copy-start.4
  88.3 0.6 copy-start.8
  88.3 0.6 copy-start.9
  88.4 0.6 copy-start.10
  89.0 35.1 %all-to-all-start.2 = ((f32[64,8,1024]{2,1,0:T(8,128)}), f32[64,8,1024]{2,1,0:T(8,128)S(1)}, u32[]{:S(2)}, u32[]{:S(2)}) async-start(f32[64,8,1024]{2,1,0:T(8,128)} %bitcast.7), calls=%async_computation.2 | async-start | bytes 4194304 | tf_op jit(solution)/shard_map/all_to_all | solution.py:487
  124.1 12.2 %collective-permute-start.7 = (f32[64,88,128]{2,1,0:T(8,128)}, f32[64,88,128]{2,1,0:T(8,128)}, u32[]{:S(2)}, u32[]{:S(2)}) collective-permute-start(f32[64,88,128]{2,1,0:T(8,128)} %get-tuple-element.83), channel_id=1, source_target_pairs={{0,32},{32,0},{1,33},{33,1},{2,34},{34,2},{3,35},{35,3},{4,36},{36... | collective-permute-start | bytes 8650760 | tf_op jit(solution)/shard_map/ppermute | solution.py:482
  127.2 38.6 %all-to-all-start.3 = ((f32[64,8,1024]{2,1,0:T(8,128)}), f32[64,8,1024]{2,1,0:T(8,128)}, u32[]{:S(2)}, u32[]{:S(2)}) async-start(f32[64,8,1024]{2,1,0:T(8,128)} %broadcast_in_dim.4), calls=%async_computation.3 | async-start | bytes 4194304 | tf_op jit(solution)/shard_map/all_to_all | solution.py:448
  212.4 43.0 %all-to-all-start.5 = ((f32[64,88,128]{2,1,0:T(8,128)}), f32[64,88,128]{2,1,0:T(8,128)S(1)}, u32[]{:S(2)}, u32[]{:S(2)}) async-start(f32[64,88,128]{2,1,0:T(8,128)} %broadcast_in_dim.5), calls=%async_computation.5 | async-start | bytes 5767168 | tf_op jit(solution)/shard_map/all_to_all | solution.py:448
  218.8 5.2 %collective-permute-start.8 = (f32[512,1024]{1,0:T(8,128)}, f32[512,1024]{1,0:T(8,128)S(1)}, u32[]{:S(2)}, u32[]{:S(2)}) collective-permute-start(f32[512,1024]{1,0:T(8,128)} %bitcast.6.mine), channel_id=1, source_target_pairs={{0,32},{32,0},{1,33},{33,1},{2,34},{34,2},{3,35},{35,3},{4,36},{36... | collective-permute-start | bytes 6291464 | tf_op jit(solution)/shard_map/ppermute | solution.py:482
  224.0 1.4 copy-start.2
  255.4 8.1 %copy-start = (f32[64,88,128]{2,1,0:T(8,128)}, f32[64,88,128]{2,1,0:T(8,128)S(1)}, u32[]{:S(2)}) copy-start(f32[64,88,128]{2,1,0:T(8,128)S(1)} %all-to-all-done.5.mine) | copy-start | bytes 8650756
  255.4 8.1 %collective-permute-start.9 = (f32[64,88,128]{2,1,0:T(8,128)S(1)}, f32[64,88,128]{2,1,0:T(8,128)S(1)}, u32[]{:S(2)}, u32[]{:S(2)}) collective-permute-start(f32[64,88,128]{2,1,0:T(8,128)S(1)} %all-to-all-done.5.mine), channel_id=1, source_target_pairs={{0,32},{32,0},{1,33},{33,1},{2,34},{34,2},{3,35},{35,3},{4,36},{36... | collective-permute-start | bytes 8650760 | tf_op jit(solution)/shard_map/ppermute | solution.py:482
  263.5 1.6 copy-start.1
